TPU v7x, 256 devices: a whole 4x4x8 slice. The times are simulated.
256 devices in a mesh: row: 8 (over z), col: 32 (over x, y, core).
Axes of the slice: x: 4, y: 4, z: 8, core: 2. Of those that a mesh axis runs over, the one named last changes fastest.
Arguments:
- frontal: float32 [8192, 65536], P('row', 'col'), may hold values from -6 to 6
- sketch: float32 [65536, 256], P('col'), may hold values from -0.0234375 to 0.0234375
- rank_table: int32 [3, 8], replicated, may hold values from 64 to 256, as said below
Outputs:
- leaf_basis: float32 [8192, 256], P(('row', 'col'))
- top_basis: float32 [8192, 256], P(('row', 'col'))
- coupling: float32 [2048, 65536], P('row', 'col')
Inputs may be any that keep to these rules, and one draw needn't show every extreme that they name: rank_table[l, g] is the rank of the level-l node made of the 2**l consecutive row groups holding g, equal over the groups of that node; a node's rank is at most the larger of its two children's ranks; in every draw some leaf has rank 256 and some leaf rank 256 // 4.
All inputs are finite; a program needn't handle non-finite values.
Results may differ from a plain program's by a relative error of at most 0.00012.
Values sent between devices are 32-bit elements; how exact they have to be, the bound alone decides.
A program may use at most 64 MiB of HBM per device.

v0:
```python
import jax
import jax.numpy as jnp
from jax import lax
from jax.sharding import PartitionSpec as P

LEVELS = 2


def swapped(block, axis, bit):
    count = lax.axis_size(axis)
    route = []
    for low in range(count):
        high = low | 1 << bit
        if high != low and high < count:
            route += [(low, high), (high, low)]
    return lax.ppermute(block, axis, route)


def product(left, right):
    return jnp.dot(left, right, precision=lax.Precision.HIGHEST, preferred_element_type=jnp.float32)


def mask_of(rank_value, width):
    return (jnp.arange(width) < rank_value).astype(jnp.float32)


def factor(gram_full, keep_mask):
    masked = keep_mask[:, None] * gram_full * keep_mask[None, :] + jnp.diag(1.0 - keep_mask)
    return jnp.linalg.cholesky(masked)


def right_solve(factor_low, operand):
    return lax.linalg.triangular_solve(
        factor_low, operand, left_side=False, lower=True, transpose_a=True
    )


def left_solve(factor_low, operand):
    return lax.linalg.triangular_solve(factor_low, operand, left_side=True, lower=True)


def body(frontal, sketch, rank_table):
    width = sketch.shape[1]
    col_count = lax.axis_size("col")
    share_rows = frontal.shape[0] // col_count
    row_group = lax.axis_index("row")
    column = lax.axis_index("col")
    keep_mask = mask_of(rank_table[0, row_group], width)
    samples = lax.psum(product(frontal, sketch), "col")
    gram_full = product(samples.T, samples)
    factor_low = factor(gram_full, keep_mask)
    full_basis = right_solve(factor_low, samples * keep_mask[None, :])
    coupling = product(full_basis.T, frontal)
    leaf_share = lax.dynamic_slice_in_dim(full_basis, column * share_rows, share_rows, 0)
    coords = left_solve(factor_low, keep_mask[:, None] * gram_full)
    chain_coef = jnp.eye(width, dtype=jnp.float32)
    for height in range(1, LEVELS + 1):
        own_gram = product(coords.T, coords)
        sibling = swapped(own_gram, "row", height - 1)
        pair_gram = own_gram + sibling
        node_mask = mask_of(rank_table[height, row_group], width)
        node_factor = factor(pair_gram, node_mask)
        chain_coef = product(chain_coef, right_solve(node_factor, coords * node_mask[None, :]))
        coords = left_solve(node_factor, node_mask[:, None] * pair_gram)
    top_share = product(leaf_share, chain_coef)
    return (leaf_share, top_share, coupling)


def solution(mesh):
    return jax.shard_map(
        body,
        mesh=mesh,
        in_specs=(P("row", "col"), P("col", None), P()),
        out_specs=(P(("row", "col"), None), P(("row", "col"), None), P("row", "col")),
        check_vma=False,
    )
```

profile of v0, /device:TPU:1, one launch (start us, length us, event | category | flops | bytes accessed | tf_op | source)
XLA Modules:
  0.0 393.3 jit_solution(1019575301217978023)
XLA Ops:
  7.2 1.5 copy-done
  8.8 10.0 %fusion.57 = f32[1024,256]{1,0:T(8,128)} fusion(f32[1024,2048]{1,0:T(8,128)} %param.8, f32[2048,256]{1,0:T(8,128)S(1)} %copy-done), kind=kOutput, calls=%fused_computation.129 | convolution fusion | flops 6442450944 | bytes 11534336 | tf_op jit(solution)/shard_map/dot_general | solution.py:20
  24.5 113.2 %all-reduce.3.cloned.1.call-done = f32[1024,256]{1,0:T(8,128)} async-done(((f32[1024,256]{1,0:T(8,128)}), f32[1024,256]{1,0:T(8,128)}) %all-reduce.3.cloned.1.call-update) | async-done | bytes 1048592 | tf_op jit(solution)/shard_map/psum | solution.py:49
  137.7 4.1 %select_add_fusion.2 = (f32[256,256]{0,1:T(8,128)S(1)}, f32[256,256]{0,1:T(8,128)}) fusion(f32[256]{0:T(256)S(1)} %broadcast_subtract_fusion.2, f32[256]{0:T(256)S(1)} %compare_convert_fusion.2, f32[1024,256]{1,0:T(8,128)} %all-reduce.3.cloned.1.call-done), kind=kOutput, calls=%fused_computation.44 | convolution fusion | flops 805634048 | bytes 1574912 | tf_op jit(solution)/shard_map/dot_general | solution.py:20
  144.4 11.7 %cholesky.172 = f32[128,128]{1,0:T(8,128)S(1)} custom-call(f32[128,128]{1,0:T(8,128)S(1)} %cholesky.270), custom_call_target="Cholesky" | custom-call | tf_op jit(solution)/shard_map/jit(cholesky)/cholesky | solution.py:29
  156.3 9.8 %custom-call.22 = f32[1,128,128]{1,2,0:T(8,128)S(1)} custom-call(f32[1,128,128]{2,1,0:T(8,128)S(1)} %get-tuple-element.98), custom_call_target="InvertDiagBlocksLowerTriangular" | custom-call | tf_op jit(solution)/shard_map/jit(cholesky)/cholesky | solution.py:29
  168.3 12.1 %cholesky.189 = f32[128,128]{1,0:T(8,128)S(1)} custom-call(f32[128,128]{1,0:T(8,128)S(1)} %convolution_subtract_fusion.6), custom_call_target="Cholesky" | custom-call | tf_op jit(solution)/shard_map/jit(cholesky)/cholesky | solution.py:29
  184.6 6.8 %while.9 = (s32[]{:T(128)}, f32[256,256]{0,1:T(8,128)S(1)}, s32[2,2]{1,0:T(2,128)}, f32[2,128,128]{2,1,0:T(8,128)}, s32[]{:T(128)}) while((s32[]{:T(128)}, f32[256,256]{0,1:T(8,128)S(1)}, s32[2,2]{1,0:T(2,128)}, f32[2,128,128]{2,1,0:T(8,128)}, s32[]{:T(128)}) %tuple.79), condition=%wide.while_cond.2, body=%wide.while_body.2.sunk | while | flops 2 | bytes 393329 | solution.py:33
  191.4 21.1 %custom-call.17 = f32[2,128,128]{1,2,0:T(8,128)} custom-call(f32[2,128,128]{2,1,0:T(8,128)} %get-tuple-element.29), custom_call_target="InvertDiagBlocksLowerTriangular" | custom-call | tf_op jit(solution)/shard_map/triangular_solve | solution.py:33
  213.8 1.9 convolution_subtract_fusion.3
  217.7 2.2 fusion.18
  226.0 10.7 %fusion = f32[256,2048]{1,0:T(8,128)} fusion(f32[1024,2048]{1,0:T(8,128)} %param.8, f32[1024,128]{0,1:T(8,128)S(1)} %fusion.42, f32[1024,128]{0,1:T(8,128)S(1)} %fusion.1), kind=kOutput, calls=%fused_computation.17 | convolution fusion | flops 6442713088 | bytes 11534336 | tf_op jit(solution)/shard_map/dot_general | solution.py:20
  238.8 11.7 %cholesky.206 = f32[128,128]{1,0:T(8,128)S(1)} custom-call(f32[128,128]{1,0:T(8,128)S(1)} %cholesky.273), custom_call_target="Cholesky" | custom-call | tf_op jit(solution)/shard_map/jit(cholesky)/cholesky | solution.py:29
  251.2 9.8 %custom-call.24 = f32[1,128,128]{1,2,0:T(8,128)S(1)} custom-call(f32[1,128,128]{2,1,0:T(8,128)S(1)} %get-tuple-element.96), custom_call_target="InvertDiagBlocksLowerTriangular" | custom-call | tf_op jit(solution)/shard_map/jit(cholesky)/cholesky | solution.py:29
  263.2 11.7 %cholesky.223 = f32[128,128]{1,0:T(8,128)S(1)} custom-call(f32[128,128]{1,0:T(8,128)S(1)} %convolution_subtract_fusion.5), custom_call_target="Cholesky" | custom-call | tf_op jit(solution)/shard_map/jit(cholesky)/cholesky | solution.py:29
  277.1 5.4 %while.10 = (s32[]{:T(128)}, f32[256,256]{1,0:T(8,128)S(1)}, s32[2,2]{1,0:T(2,128)}, f32[2,128,128]{2,1,0:T(8,128)S(1)}, s32[]{:T(128)}) while((s32[]{:T(128)}, f32[256,256]{1,0:T(8,128)S(1)}, s32[2,2]{1,0:T(2,128)}, f32[2,128,128]{2,1,0:T(8,128)S(1)}, s32[]{:T(128)}) %tuple.82), condition=%wide.while_cond.1, body=%wide.while_body.1.sunk | while | flops 2 | bytes 131189 | solution.py:33
  282.5 19.7 %custom-call.25 = f32[2,128,128]{1,2,0:T(8,128)S(1)} custom-call(f32[2,128,128]{2,1,0:T(8,128)S(1)} %get-tuple-element.43), custom_call_target="InvertDiagBlocksLowerTriangular" | custom-call | tf_op jit(solution)/shard_map/triangular_solve/custom-call.5 | solution.py:33
  304.3 2.6 collective-permute-start.1
  307.5 11.7 %collective-permute-done.1 = f32[256,256]{0,1:T(8,128)S(1)} collective-permute-done((f32[256,256]{0,1:T(8,128)S(1)}, f32[256,256]{0,1:T(8,128)S(1)}, u32[]{:S(2)}, u32[]{:S(2)}) %collective-permute-start.1) | collective-permute-done | bytes 262176 | tf_op jit(solution)/shard_map/ppermute | solution.py:16
  320.2 11.7 %cholesky.240 = f32[128,128]{1,0:T(8,128)S(1)} custom-call(f32[128,128]{1,0:T(8,128)S(1)} %cholesky.276), custom_call_target="Cholesky" | custom-call | tf_op jit(solution)/shard_map/jit(cholesky)/cholesky | solution.py:29
  332.7 9.8 %custom-call.27 = f32[1,128,128]{1,2,0:T(8,128)S(1)} custom-call(f32[1,128,128]{2,1,0:T(8,128)S(1)} %get-tuple-element.92), custom_call_target="InvertDiagBlocksLowerTriangular" | custom-call | tf_op jit(solution)/shard_map/jit(cholesky)/cholesky | solution.py:29
  344.7 11.7 %cholesky.257 = f32[128,128]{1,0:T(8,128)S(1)} custom-call(f32[128,128]{1,0:T(8,128)S(1)} %convolution_subtract_fusion.4), custom_call_target="Cholesky" | custom-call | tf_op jit(solution)/shard_map/jit(cholesky)/cholesky | solution.py:29
  358.5 5.7 %while.11 = (s32[]{:T(128)}, f32[256,256]{1,0:T(8,128)S(1)}, s32[2,2]{1,0:T(2,128)}, f32[2,128,128]{2,1,0:T(8,128)S(1)}, s32[]{:T(128)}) while((s32[]{:T(128)}, f32[256,256]{1,0:T(8,128)S(1)}, s32[2,2]{1,0:T(2,128)}, f32[2,128,128]{2,1,0:T(8,128)S(1)}, s32[]{:T(128)}) %tuple.85), condition=%wide.while_cond.1.clone, body=%wide.while_body.1.clone.sunk | while | flops 2 | bytes 131189 | solution.py:33
  364.2 19.7 %custom-call.28 = f32[2,128,128]{1,2,0:T(8,128)S(1)} custom-call(f32[2,128,128]{2,1,0:T(8,128)S(1)} %get-tuple-element.45), custom_call_target="InvertDiagBlocksLowerTriangular" | custom-call | tf_op jit(solution)/shard_map/triangular_solve/custom-call.5 | solution.py:33
  (117 shorter events, 55.6 us)
Async XLA Ops:
  7.2 1.6 copy-start
  7.2 11.6 %copy-start.7 = (s32[3,8]{1,0:T(4,128)S(1)}, s32[3,8]{1,0:T(4,128)}, u32[]{:S(2)}) copy-start(s32[3,8]{1,0:T(4,128)} %param.10) | copy-start | bytes 292
  7.2 130.5 %all-reduce.3.cloned.1.call-start = ((), (), s32[]{:S(2)}) async-start(), calls=%async_computation | async-start | bytes 2097152 | tf_op jit(solution)/shard_map/psum | solution.py:49
  137.7 83.4 %copy-start.1 = (f32[1024,256]{1,0:T(8,128)S(1)}, f32[1024,256]{1,0:T(8,128)}, u32[]{:S(2)}) copy-start(f32[1024,256]{1,0:T(8,128)} %all-reduce.3.cloned.1.call-done) | copy-start | bytes 3145732
  143.7 0.7 copy-start.4
  217.7 6.0 %copy-start.2 = (f32[128,256]{0,1:T(8,128)}, f32[128,256]{0,1:T(8,128)S(1)}, u32[]{:S(2)}) copy-start(f32[128,256]{0,1:T(8,128)S(1)} %fusion.41) | copy-start | bytes 393220
  219.8 16.8 %collective-permute-start = (f32[256,256]{0,1:T(8,128)}, f32[256,256]{0,1:T(8,128)}, u32[]{:S(2)}, u32[]{:S(2)}) collective-permute-start(f32[256,256]{0,1:T(8,128)} %fusion.18), channel_id=1, source_target_pairs={{0,32},{32,0},{64,96},{96,64},{128,160},{160,128},{192,224},{224,1... | collective-permute-start | bytes 786440 | tf_op jit(solution)/shard_map/ppermute | solution.py:16
  221.2 15.5 %copy-start.8 = (f32[256]{0:T(256)S(1)}, f32[256]{0:T(256)}, u32[]{:S(2)}) copy-start(f32[256]{0:T(256)} %broadcast_subtract_fusion.1) | copy-start | bytes 3076
  225.2 11.5 %copy-start.3 = (f32[128,256]{0,1:T(8,128)S(1)}, f32[128,256]{0,1:T(8,128)}, u32[]{:S(2)}) copy-start(f32[128,256]{0,1:T(8,128)} %copy-done.2) | copy-start | bytes 393220
  238.1 0.7 copy-start.5
  304.3 15.0 %collective-permute-start.1 = (f32[256,256]{0,1:T(8,128)S(1)}, f32[256,256]{0,1:T(8,128)S(1)}, u32[]{:S(2)}, u32[]{:S(2)}) collective-permute-start(f32[256,256]{0,1:T(8,128)S(1)} %fusion.16), channel_id=1, source_target_pairs={{0,64},{64,0},{32,96},{96,32},{128,192},{192,128},{160,224},{224,1... | collective-permute-start | bytes 786440 | tf_op jit(solution)/shard_map/ppermute | solution.py:16
  319.5 0.7 copy-start.6
Sparse Core Ops, SparseCore 0:
  18.9 118.7 all-reduce.2
where the time goes:
time: 398 us; the launch traced here: 393 us
  other arithmetic  172 us (43%)
  waiting for transfers between devices  125 us (31%)
  matrix products  46.7 us (12%)
  local copies, waits for them, and re-layouts  26.8 us (7%)
  between operations  18.8 us (5%)
    psum x1, waiting for transfers between devices, body(): samples = lax.psum(product(frontal, sketch), 'col')  113 us
    another operation x20, other arithmetic, factor(): return jnp.linalg.cholesky(masked)  104 us
    another operation x8, other arithmetic, right_solve(): lax.linalg.triangular_solve(factor_low, operand, left_side=False, lower=T...  61.2 us
    dot_general x8, matrix products, product(): jnp.dot(left, right, precision=lax.Precision.HIGHEST, preferred_element_t...  29.1 us
    another operation x13, local copies, waits for them, and re-layouts, right_solve(): lax.linalg.triangular_solve(factor_low, operand, left_side=False, lower=T...  12 us
    ppermute x2, waiting for transfers between devices, swapped(): return lax.ppermute(block, axis, route)  11.7 us
  transfers between devices with their start and end apart: 3, of which 2 were waited for; matrix products, arithmetic and copies ran while one was open for 6% of the time, Pallas kernels for 0%

commit v1 on v0

v1 whole, which is shorter than its diff:
```python
import functools

import jax
import jax.numpy as jnp
from jax import lax
from jax.experimental import pallas as pl
from jax.experimental.pallas import tpu as pltpu
from jax.sharding import PartitionSpec as P

MESH = pl.DeviceIdType.MESH
NN = (((1,), (0,)), ((), ()))
NT = (((1,), (1,)), ((), ()))
TN = (((0,), (0,)), ((), ()))
PB = 32
F32 = jnp.float32


def split(x):
    hi = x.astype(jnp.bfloat16)
    return hi, (x - hi.astype(F32)).astype(jnp.bfloat16)


def dot3(a, b, dims=NN):
    ah, al = a if isinstance(a, tuple) else split(a)
    bh, bl = b if isinstance(b, tuple) else split(b)
    d = functools.partial(lax.dot_general, dimension_numbers=dims, preferred_element_type=F32)
    return d(ah, bh) + (d(ah, bl) + d(al, bh))


def diag_inverse(x):
    lane = lax.broadcasted_iota(jnp.int32, (8, 128), 1)
    sub = lax.broadcasted_iota(jnp.int32, (8, 128), 0)
    base = (lane // PB) * PB
    n = [jnp.where(lane % PB == sub + 8 * g, 1.0, 0.0).astype(jnp.float32) for g in range(4)]
    m = list(x)
    scale = [jnp.zeros((8, 128), jnp.float32) for _ in range(4)]
    for q in range(4):
        c = {}
        for k in range(8):
            for g in range(q, 4):
                c[k, g] = jnp.take_along_axis(m[g], base + (8 * q + k), axis=1)
        for j in range(8):
            def row(v):
                return jnp.broadcast_to(v[j:j + 1, :], (8, 128))
            p = row(c[j, q])
            rs = lax.rsqrt(p)
            r = rs * rs
            scale[q] = jnp.where(sub == j, rs, scale[q])
            crow = {k: row(c[k, q]) for k in range(j + 1, 8)}
            mrow = row(m[q]) if q < 3 else None
            nrow = row(n[q])
            for g in range(q, 4):
                f = c[j, g] * r
                if g == q:
                    f = jnp.where(sub > j, f, 0.0)
                for k in range(j + 1, 8):
                    c[k, g] = c[k, g] - f * crow[k]
                if q < 3:
                    m[g] = m[g] - f * mrow
                n[g] = n[g] - f * nrow
    return [n[g] * scale[g] for g in range(4)]

def chol_inverse(z_ref, batch, count=256):
    def tile_step(t, _):
        lane0 = pl.multiple_of(t * 128, 128)
        for s in range(128 // PB):
            start = pl.multiple_of(t * 128 + s * PB, PB)
            lane = lax.broadcasted_iota(jnp.int32, (8, 128), 1)
            packed = []
            for g in range(4):
                v = None
                for b in range(4):
                    bb = b if b < batch else 0
                    d = z_ref[bb, pl.ds(start + 8 * g, 8), pl.ds(lane0, 128)]
                    shift = (PB * b - PB * s) % 128
                    if shift:
                        d = pltpu.roll(d, shift, 1)
                    v = d if v is None else jnp.where(lane // PB == b, d, v)
                packed.append(v)
            w4 = jnp.concatenate(diag_inverse(packed), axis=0)
            rows = lax.broadcasted_iota(jnp.int32, (256, 1), 0)
            lanes = lax.broadcasted_iota(jnp.int32, (1, 256), 1)
            incol = (lanes >= start) & (lanes < start + PB)
            eye = (lax.broadcasted_iota(jnp.int32, (PB, 256), 1) == lax.broadcasted_iota(jnp.int32, (PB, 256), 0) + start)
            for b in range(batch):
                w = split(w4[:, PB * b:PB * (b + 1)])
                r = z_ref[b, pl.ds(start, PB), :]
                r = jnp.where(incol, eye.astype(jnp.float32), r)
                u = dot3(w, split(r))
                zc = z_ref[b, :, pl.ds(lane0, 128)][:, PB * s:PB * (s + 1)]
                lm = dot3(split(zc), w, NT)
                lm = jnp.where(rows >= start + PB, lm, 0.0)
                z = z_ref[b]
                z = jnp.where(incol & (rows >= start), 0.0, z)
                z_ref[b] = z - dot3(split(lm), split(u))
                z_ref[b, pl.ds(start, PB), :] = u
        return 0
    lax.fori_loop(0, 2, tile_step, 0)
    r = lax.broadcasted_iota(jnp.int32, (256, 256), 0)
    cc = lax.broadcasted_iota(jnp.int32, (256, 256), 1)
    for b in range(batch):
        z_ref[b] = jnp.where(cc <= r, z_ref[b], 0.0)

def gather_kernel(f_hbm, s_hbm, samples, grams, fbuf, sbuf, sh, sl, part, xbuf, outbuf, rbuf, acc,
                  fsem, ssem, xs_sem, xr_sem, rs_sem, rr_sem, as_sem, ar_sem, ws_sem, wr_sem,
                  zs_sem, zr_sem, gs_sem, gr_sem, hs_sem, hr_sem):
    z = lax.axis_index("row")
    me = lax.axis_index("col")
    core = lax.rem(me, 2)
    chip = lax.div(me, 2)
    x = lax.div(chip, 4)
    y = lax.rem(chip, 4)
    quad = lax.div(z, 4) * 4
    zq = lax.rem(z, 4)
    sibling = {"row": z, "col": chip * 2 + 1 - core}

    def peer(q):
        return {"row": z, "col": q * 2 + core}

    def along_z(m):
        return {"row": quad + m, "col": me}

    def chunk_copy(s):
        rows = pl.multiple_of(lax.rem(x + 1 + s, 4) * 256, 256)
        return pltpu.make_async_copy(f_hbm.at[pl.ds(rows, 256)], fbuf.at[s], fsem.at[s])

    scopy = pltpu.make_async_copy(s_hbm, sbuf, ssem)
    scopy.start()
    for s in range(4):
        chunk_copy(s).start()

    barrier = pltpu.get_barrier_semaphore()
    pl.semaphore_signal(barrier, inc=1, device_id=sibling, device_id_type=MESH)

    @pl.loop(1, 16)
    def _(t):
        pl.semaphore_signal(barrier, inc=1, device_id=peer(lax.rem(chip + t, 16)), device_id_type=MESH)

    for t in range(1, 4):
        pl.semaphore_signal(barrier, inc=1, device_id=along_z(lax.rem(zq + t, 4)), device_id_type=MESH)

    scopy.wait()
    sh[...], sl[...] = split(sbuf[...])
    pl.semaphore_wait(barrier, 19)

    def remote(src, dst, send, recv, device):
        return pltpu.make_async_remote_copy(src_ref=src, dst_ref=dst, send_sem=send, recv_sem=recv,
                                            device_id=device, device_id_type=MESH)

    def cores_copy(s):
        return remote(part.at[s, :, 1 - core], xbuf.at[s], xs_sem.at[s], xr_sem.at[s], sibling)

    def shard_copy(s, yy, q):
        return remote(outbuf.at[s, yy], rbuf.at[chip], rs_sem.at[q], rr_sem.at[chip], peer(q))

    @pl.loop(0, 5)
    def _(s):
        @pl.when(s < 4)
        def _():
            chunk_copy(s).wait()
            p = dot3(split(fbuf[s]), (sh[...], sl[...]))
            part[s] = p.reshape(4, 2, 32, 256)
            cores_copy(s).start()

        @pl.when(s > 0)
        def _():
            t = s - 1
            xt = lax.rem(x + 1 + t, 4)
            cores_copy(t).wait_recv()
            outbuf[t] = part[t, :, core] + xbuf[t]

            @pl.loop(0, 4)
            def _(u):
                yy = lax.rem(y + 1 + u, 4)
                q = xt * 4 + yy

                @pl.when(q != chip)
                def _():
                    shard_copy(t, yy, q).start()

    acc[...] = outbuf[3, y]

    @pl.loop(1, 16)
    def _(t):
        q = lax.rem(chip + t, 16)
        remote(outbuf.at[0, 0], rbuf.at[q], rs_sem.at[q], rr_sem.at[q], peer(q)).wait_recv()
        acc[...] += rbuf[q]

    samples[me] = acc[...]

    def own_copy(q):
        return remote(samples.at[me], samples.at[me], as_sem.at[q], ar_sem.at[chip], peer(q))

    def relay_copy(q):
        return remote(samples.at[q * 2 + core], samples.at[q * 2 + core], ws_sem.at[q], wr_sem.at[q], sibling)

    @pl.loop(1, 16)
    def _(t):
        own_copy(lax.rem(chip + t, 16)).start()

    relay_copy(chip).start()

    @pl.loop(1, 16)
    def _(t):
        q = lax.rem(chip + 16 - t, 16)
        remote(samples.at[me], samples.at[q * 2 + core], as_sem.at[q], ar_sem.at[q], peer(q)).wait_recv()
        relay_copy(q).start()

    @pl.loop(0, 16)
    def _(q):
        remote(samples.at[q * 2 + core], samples.at[q * 2 + 1 - core], ws_sem.at[q], wr_sem.at[q], sibling).wait_recv()

    full = split(samples[...].reshape(1024, 256))
    grams[0] = dot3(full, full, TN).reshape(32, 8, 256)

    def z_copy(t):
        return remote(grams.at[0, me], grams.at[t, me], zs_sem.at[t], zr_sem.at[t], along_z(lax.rem(zq + 4 - t, 4)))

    for t in range(1, 4):
        z_copy(t).start()
    for t in range(1, 4):
        z_copy(t).wait_recv()

    def gram_slice(c):
        return grams.at[pl.ds(1, 3), c]

    def gram_copy(q):
        return remote(gram_slice(me), gram_slice(me), gs_sem.at[q], gr_sem.at[chip], peer(q))

    def gram_relay(q):
        return remote(gram_slice(q * 2 + core), gram_slice(q * 2 + core), hs_sem.at[q], hr_sem.at[q], sibling)

    @pl.loop(1, 16)
    def _(t):
        gram_copy(lax.rem(chip + t, 16)).start()

    gram_relay(chip).start()

    @pl.loop(1, 16)
    def _(t):
        q = lax.rem(chip + 16 - t, 16)
        remote(gram_slice(me), gram_slice(q * 2 + core), gs_sem.at[q], gr_sem.at[q], peer(q)).wait_recv()
        gram_relay(q).start()

    @pl.loop(0, 16)
    def _(q):
        remote(gram_slice(q * 2 + core), gram_slice(q * 2 + 1 - core), hs_sem.at[q], hr_sem.at[q], sibling).wait_recv()

    for s in range(4):
        cores_copy(s).wait_send()
    for t in range(1, 4):
        z_copy(t).wait_send()

    @pl.loop(1, 16)
    def _(t):
        q = lax.rem(chip + t, 16)
        shard_copy(0, 0, q).wait_send()
        own_copy(q).wait_send()
        gram_copy(q).wait_send()

    @pl.loop(0, 16)
    def _(q):
        relay_copy(q).wait_send()
        gram_relay(q).wait_send()


def gathered(frontal, sketch):
    vmem = pl.BlockSpec(memory_space=pltpu.VMEM)
    hbm = pl.BlockSpec(memory_space=pl.ANY)
    dma = pltpu.SemaphoreType.DMA
    return pl.pallas_call(
        gather_kernel,
        out_shape=(jax.ShapeDtypeStruct((32, 32, 256), F32), jax.ShapeDtypeStruct((4, 32, 8, 256), F32)),
        in_specs=[hbm, hbm],
        out_specs=(vmem, vmem),
        scratch_shapes=[
            pltpu.VMEM((4, 256, 2048), F32),
            pltpu.VMEM((2048, 256), F32),
            pltpu.VMEM((2048, 256), jnp.bfloat16),
            pltpu.VMEM((2048, 256), jnp.bfloat16),
            pltpu.VMEM((4, 4, 2, 32, 256), F32),
            pltpu.VMEM((4, 4, 32, 256), F32),
            pltpu.VMEM((4, 4, 32, 256), F32),
            pltpu.VMEM((16, 32, 256), F32),
            pltpu.VMEM((32, 256), F32),
            dma((4,)), dma, dma((4,)), dma((4,)),
            dma((16,)), dma((16,)), dma((16,)), dma((16,)), dma((16,)), dma((16,)),
            dma((4,)), dma((4,)), dma((16,)), dma((16,)), dma((16,)), dma((16,)),
        ],
        compiler_params=pltpu.CompilerParams(collective_id=0, has_side_effects=True, vmem_limit_bytes=40 * 2**20),
        cost_estimate=pl.CostEstimate(flops=3 * 2**30, bytes_accessed=10 * 2**20, transcendentals=0),
    )(frontal, sketch)


def masked(gram, rank):
    r = lax.broadcasted_iota(jnp.int32, (256, 256), 0)
    c = lax.broadcasted_iota(jnp.int32, (256, 256), 1)
    return jnp.where((r < rank) & (c < rank), gram, jnp.where(r == c, 1.0, 0.0))


def row_masked(a, rank):
    return jnp.where(lax.broadcasted_iota(jnp.int32, a.shape, 0) < rank, a, 0.0)


def col_masked(a, rank):
    return jnp.where(lax.broadcasted_iota(jnp.int32, a.shape, 1) < rank, a, 0.0)


def tree_kernel(ranks, samples, grams, f_hbm, leaf, top, coupling, fbuf, zb, cb, tb, pairs, fsem):
    z = lax.axis_index("row")
    me = lax.axis_index("col")
    quad = lax.div(z, 4) * 4
    zq = lax.rem(z, 4)
    fcopy = pltpu.make_async_copy(f_hbm, fbuf, fsem)
    fcopy.start()

    def gram(m):
        return grams[lax.rem(m + 4 - zq, 4)]

    for m in range(4):
        zb[m] = masked(gram(m), ranks[0, quad + m])
    chol_inverse(zb, 4)
    r0 = ranks[0, z]
    w_own = split(zb[zq])
    share = dot3(split(col_masked(samples[pl.ds(pl.multiple_of(me * 32, 32), 32), :], r0)), w_own, NT)
    leaf[...] = share
    for m in range(4):
        rank = ranks[0, quad + m]
        w = split(zb[m])
        g = gram(m)
        cb[m] = dot3(w, split(row_masked(g, rank)))
        tb[m] = dot3(split(col_masked(g, rank)), w, NT)
    chain = dot3(split(share), split(cb[zq]))
    basis_t = dot3(w_own, split(col_masked(samples[...], r0)), NT)
    for n in range(2):
        pairs[n] = dot3(split(tb[2 * n]), split(cb[2 * n])) + dot3(split(tb[2 * n + 1]), split(cb[2 * n + 1]))
        zb[n] = masked(pairs[n], ranks[1, quad + 2 * n])
    chol_inverse(zb, 2)
    own = lax.div(zq, 2)
    chain = dot3(split(col_masked(chain, ranks[1, z])), split(zb[own]), NT)
    for n in range(2):
        rank = ranks[1, quad + 2 * n]
        w = split(zb[n])
        g = pairs[n]
        cb[n] = dot3(w, split(row_masked(g, rank)))
        tb[n] = dot3(split(col_masked(g, rank)), w, NT)
    chain = dot3(split(chain), split(cb[own]))
    zb[0] = masked(dot3(split(tb[0]), split(cb[0])) + dot3(split(tb[1]), split(cb[1])), ranks[2, quad])
    chol_inverse(zb, 1)
    top[...] = dot3(split(col_masked(chain, ranks[2, z])), split(zb[0]), NT)
    fcopy.wait()
    bt = split(basis_t)

    @pl.loop(0, 8)
    def _(i):
        cols = pl.ds(pl.multiple_of(i * 256, 256), 256)
        coupling[:, cols] = dot3(bt, split(fbuf[:, cols]))


def tree(ranks, samples, grams, frontal):
    vmem = pl.BlockSpec(memory_space=pltpu.VMEM)
    return pl.pallas_call(
        tree_kernel,
        out_shape=(jax.ShapeDtypeStruct((32, 256), F32), jax.ShapeDtypeStruct((32, 256), F32),
                   jax.ShapeDtypeStruct((256, 2048), F32)),
        in_specs=[pl.BlockSpec(memory_space=pltpu.SMEM), vmem, vmem, pl.BlockSpec(memory_space=pl.ANY)],
        out_specs=(vmem, vmem, vmem),
        scratch_shapes=[
            pltpu.VMEM((1024, 2048), F32),
            pltpu.VMEM((4, 256, 256), F32),
            pltpu.VMEM((4, 256, 256), F32),
            pltpu.VMEM((4, 256, 256), F32),
            pltpu.VMEM((2, 256, 256), F32),
            pltpu.SemaphoreType.DMA,
        ],
        compiler_params=pltpu.CompilerParams(vmem_limit_bytes=48 * 2**20),
        cost_estimate=pl.CostEstimate(flops=4 * 2**30, bytes_accessed=12 * 2**20, transcendentals=0),
    )(ranks, samples, grams, frontal)


def body(frontal, sketch, rank_table):
    samples, grams = gathered(frontal, sketch)
    return tree(rank_table, samples.reshape(1024, 256), grams.reshape(4, 256, 256), frontal)


def solution(mesh):
    return jax.shard_map(
        body,
        mesh=mesh,
        in_specs=(P("row", "col"), P("col", None), P()),
        out_specs=(P(("row", "col"), None), P(("row", "col"), None), P("row", "col")),
        check_vma=False,
    )
```

time: 398 us -> 115 us (0.29); the launches traced: 393 us -> 115 us
  other arithmetic: 172 us -> 0 us
  waiting for transfers between devices: 125 us -> 0 us
  Pallas kernels: 0 us -> 109 us
  matrix products: 46.7 us -> 0 us
  local copies, waits for them, and re-layouts: 26.8 us -> 4.97 us
  between operations: 18.8 us -> 0.82 us
    another operation x28 -> x0, other arithmetic: 165 us -> none  [the longest x20 104 us: factor(): return jnp.linalg.cholesky(masked)]
    psum x1 -> x0, waiting for transfers between devices: 113 us -> none  [body(): samples = lax.psum(product(frontal, sketch), 'col')]
    pallas_call x0 -> x2, Pallas kernels: none -> 109 us  [the longest x1 62.1 us: tree(): pl.pallas_call(tree_kernel, out_shape=(jax.ShapeDtypeStruct((32, 256), F3...]
    dot_general x8 -> x0, matrix products: 29.1 us -> none  [product(): jnp.dot(left, right, precision=lax.Precision.HIGHEST, preferred_element_t...]
    another operation x36 -> x0, local copies, waits for them, and re-layouts: 20 us -> none  [the longest x13 12 us: right_solve(): lax.linalg.triangular_solve(factor_low, operand, left_side=False, lower=T...]
    another operation x21 -> x0, matrix products: 17.5 us -> none  [the longest x6 6.45 us: factor(): return jnp.linalg.cholesky(masked)]
    ppermute x2 -> x0, waiting for transfers between devices: 11.7 us -> none  [swapped(): return lax.ppermute(block, axis, route)]
  transfers between devices with their start and end apart: 3 -> 0, of which waited for: 2 -> 0; matrix products, arithmetic and copies ran while one was open for 6% -> 0% of each run, Pallas kernels for 0% -> 0%
where the time goes in v1:
time: 115 us
  Pallas kernels  109 us (95%)
  local copies, waits for them, and re-layouts  4.97 us (4%)
    pallas_call x1, Pallas kernels, tree(): pl.pallas_call(tree_kernel, out_shape=(jax.ShapeDtypeStruct((32, 256), F3...  62.1 us
    pallas_call x1, Pallas kernels, gathered(): pl.pallas_call(gather_kernel, out_shape=(jax.ShapeDtypeStruct((32, 32, 25...  47.1 us
    unnamed x6, local copies, waits for them, and re-layouts  4.97 us

profile of v1, /device:TPU:1, one launch (start us, length us, event | category | flops | bytes accessed | tf_op | source)
XLA Modules:
  0.0 115.0 jit_solution(2299664579229483125)
XLA Ops:
  0.6 0.0 copy-start
  0.6 3.4 %copy-done = f32[1024,2048]{1,0:T(8,128)S(1)} copy-done((f32[1024,2048]{1,0:T(8,128)S(1)}, f32[1024,2048]{1,0:T(8,128)}, u32[]{:S(2)}) %copy-start) | copy-done | bytes 8388632
  4.0 0.0 copy-start.1
  4.0 1.6 %copy-done.1 = f32[2048,256]{1,0:T(8,128)S(1)} copy-done((f32[2048,256]{1,0:T(8,128)S(1)}, f32[2048,256]{1,0:T(8,128)}, u32[]{:S(2)}) %copy-start.1) | copy-done | bytes 2097176
  5.6 0.0 copy-start.2
  5.6 47.1 %shard_map.58 = (f32[32,32,256]{2,1,0:T(8,128)S(1)}, f32[4,32,8,256]{3,2,1,0:T(8,128)S(1)}) custom-call(f32[1024,2048]{1,0:T(8,128)S(1)} %copy-done, f32[2048,256]{1,0:T(8,128)S(1)} %copy-done.1), custom_call_target="tpu_custom_call" | custom-call | flops 3221225472 | bytes 10485760 | tf_op jit(solution)/shard_map/pallas_call | solution.py:271
  52.7 0.0 copy-done.2
  52.7 62.1 %shard_map.59 = (f32[32,256]{1,0:T(8,128)}, f32[32,256]{1,0:T(8,128)}, f32[256,2048]{1,0:T(8,128)}) custom-call(s32[3,8]{1,0:T(4,128)S(1)} %copy-done.2, f32[1024,256]{1,0:T(8,128)S(1)} %bitcast.2, f32[4,256,256]{2,1,0:T(8,128)S(1)} %bitcast.3, f32[1024,2048]{1,0:T(8,128)} %f_hbm.3), custom_call_target="tpu_custom_call" | custom-call | flops 4294967296 | bytes 12582912 | tf_op jit(solution)/shard_map/pallas_call | solution.py:362
Async XLA Ops:
  0.6 3.4 %copy-start = (f32[1024,2048]{1,0:T(8,128)S(1)}, f32[1024,2048]{1,0:T(8,128)}, u32[]{:S(2)}) copy-start(f32[1024,2048]{1,0:T(8,128)} %f_hbm.3) | copy-start | bytes 25165828
  4.0 1.6 %copy-start.1 = (f32[2048,256]{1,0:T(8,128)S(1)}, f32[2048,256]{1,0:T(8,128)}, u32[]{:S(2)}) copy-start(f32[2048,256]{1,0:T(8,128)} %s_hbm.1) | copy-start | bytes 6291460
  5.6 47.1 %copy-start.2 = (s32[3,8]{1,0:T(4,128)S(1)}, s32[3,8]{1,0:T(4,128)}, u32[]{:S(2)}) copy-start(s32[3,8]{1,0:T(4,128)} %ranks.1) | copy-start | bytes 292

commit v2 on v0

v2 whole, which is shorter than its diff:
```python
import functools

import jax
import jax.numpy as jnp
from jax import lax
from jax.experimental import pallas as pl
from jax.experimental.pallas import tpu as pltpu
from jax.sharding import PartitionSpec as P

MESH = pl.DeviceIdType.MESH
NN = (((1,), (0,)), ((), ()))
NT = (((1,), (1,)), ((), ()))
TN = (((0,), (0,)), ((), ()))
F32 = jnp.float32


def split(x):
    hi = x.astype(jnp.bfloat16)
    return hi, (x - hi.astype(F32)).astype(jnp.bfloat16)


def dot3(a, b, dims=NN):
    ah, al = a if isinstance(a, tuple) else split(a)
    bh, bl = b if isinstance(b, tuple) else split(b)
    d = functools.partial(lax.dot_general, dimension_numbers=dims, preferred_element_type=F32)
    return d(ah, bh) + (d(ah, bl) + d(al, bh))


PB = 32
HALF = 16


def diag_inverse(x):
    lane = lax.broadcasted_iota(jnp.int32, (8, 128), 1)
    sub = lax.broadcasted_iota(jnp.int32, (8, 128), 0)
    base = (lane // PB) * PB
    m = list(x)
    n = [jnp.where(lane % PB == sub + 8 * g, 1.0, 0.0).astype(F32) for g in range(4)]
    scale = [jnp.zeros((8, 128), F32) for _ in range(4)]
    coef = [jnp.zeros((8, 128), F32) for _ in range(4)]
    for q in range(2):
        c = {}
        for k in range(HALF):
            for g in range(2 * q, 4):
                c[k, g] = jnp.take_along_axis(m[g], base + (HALF * q + k), axis=1)
        for j in range(0, HALF, 2):
            gj = 2 * q + j // 8
            s0 = j % 8

            def row(v, i):
                return jnp.broadcast_to(v[i:i + 1, :], (8, 128))

            a = row(c[j, gj], s0)
            b = row(c[j, gj], s0 + 1)
            d = row(c[j + 1, gj], s0 + 1)
            det = a * d - b * b
            rdet = 1.0 / det
            ra = 1.0 / a
            scale[gj] = jnp.where(sub == s0, lax.rsqrt(a), jnp.where(sub == s0 + 1, lax.rsqrt(det * ra), scale[gj]))
            coef[gj] = jnp.where(sub == s0 + 1, b * ra, coef[gj])
            first = {k: row(c[k, gj], s0) for k in range(j + 2, HALF)}
            second = {k: row(c[k, gj], s0 + 1) for k in range(j + 2, HALF)}
            n0, n1 = row(n[gj], s0), row(n[gj], s0 + 1)
            m0, m1 = row(m[gj], s0), row(m[gj], s0 + 1)
            for g in range(gj, 4):
                if g == gj and s0 == 6:
                    continue
                e = d * c[j, g] - b * c[j + 1, g]
                f = a * c[j + 1, g] - b * c[j, g]
                if g == gj:
                    e = jnp.where(sub > s0 + 1, e, 0.0)
                    f = jnp.where(sub > s0 + 1, f, 0.0)
                e = e * rdet
                f = f * rdet
                for k in range(j + 2, HALF):
                    c[k, g] = c[k, g] - (e * first[k] + f * second[k])
                if q == 0:
                    m[g] = m[g] - (e * m0 + f * m1)
                n[g] = n[g] - (e * n0 + f * n1)
    return [(n[g] - coef[g] * pltpu.roll(n[g], 1, 0)) * scale[g] for g in range(4)]


def place(z_ref, b, a):
    for t in range(2):
        cols = a[:, 128 * t:128 * t + 128]
        if b:
            cols = pltpu.roll(cols, 32 * b, 1)
        for s in range(8):
            dst = 128 * (s // 4) + 32 * ((s + b) % 4)
            z_ref[b, dst:dst + 32, 128 * t:128 * t + 128] = cols[32 * s:32 * s + 32]


def taken(z_ref, b):
    tiles = []
    for t in range(2):
        cols = jnp.concatenate([
            z_ref[b, 128 * (s // 4) + 32 * ((s + b) % 4):128 * (s // 4) + 32 * ((s + b) % 4) + 32, 128 * t:128 * t + 128]
            for s in range(8)], axis=0)
        if b:
            cols = pltpu.roll(cols, 128 - 32 * b, 1)
        tiles.append(cols)
    w = jnp.concatenate(tiles, axis=1)
    r = lax.broadcasted_iota(jnp.int32, (256, 256), 0)
    c = lax.broadcasted_iota(jnp.int32, (256, 256), 1)
    return jnp.where(c <= r, w, 0.0)


def chol_inverse(z_ref, batch, work=None):
    lane8 = lax.broadcasted_iota(jnp.int32, (8, 128), 1)
    lane = lax.broadcasted_iota(jnp.int32, (PB, 128), 1)
    lane96 = lax.broadcasted_iota(jnp.int32, (1, 96), 1)
    zeros = jnp.zeros((PB, 256), jnp.bfloat16)
    d = functools.partial(lax.dot_general, preferred_element_type=F32)
    for p in range(8):
        t, s = p // 4, p % 4
        tile = slice(128 * t, 128 * t + 128)
        packed = []
        for g in range(4):
            v = None
            for b in range(batch):
                at = 128 * t + 32 * ((s + b) % 4) + 8 * g
                blk = z_ref[b, at:at + 8, tile]
                v = blk if v is None else jnp.where(lane8 // PB == (s + b) % 4, blk, v)
            packed.append(v)
        w4 = jnp.concatenate(diag_inverse(packed), axis=0)
        for b in range(batch):
            turn = (s + b) % 4
            start = 128 * t + 32 * turn
            here = lane // PB == turn
            w = jnp.where(here, w4, 0.0)
            wh, wl = split(w)
            rh, rl = split(z_ref[b, start:start + PB, :])

            def padded(v):
                return jnp.concatenate([zeros] * turn + [v] + [zeros] * (3 - turn), axis=0)

            ph = padded(rh)
            u = d(wh, ph, NN) + (d(wl, ph, NN) + d(wh, padded(rl), NN))
            ut = [u[:, :128], u[:, 128:]]
            ut[t] = jnp.where(here, w4, ut[t])
            u = jnp.concatenate(ut, axis=1)
            z_ref[b, start:start + PB, :] = u
            left = [128 * (i // 4) + 32 * ((i % 4 + b) % 4) for i in range(p + 1, 8)]
            if not left:
                continue
            zt = jnp.concatenate([z_ref[b, r:r + PB, tile] for r in left], axis=0)
            zh, zl = split(zt)
            wh3 = jnp.concatenate([wh] * 3, axis=0)
            wl3 = jnp.concatenate([wl] * 3, axis=0)
            lm = d(jnp.concatenate([zh, zl], axis=1), jnp.concatenate([wh3, wh3], axis=1), NT) + d(zh, wl3, NT)
            lh, ll = split(lm)
            l96 = jnp.where(lane96 < 64, lh, ll)
            uh, ul = split(u)
            delta = d(l96, jnp.concatenate([uh, ul, uh], axis=0), NN)
            for i, r in enumerate(left):
                rows = slice(PB * i, PB * i + PB)
                for tt in range(2):
                    cols = slice(128 * tt, 128 * tt + 128)
                    old = z_ref[b, r:r + PB, cols]
                    if tt == t:
                        old = jnp.where(here, 0.0, old)
                    z_ref[b, r:r + PB, cols] = old - delta[rows, cols]


def masked(gram, rank):
    r = lax.broadcasted_iota(jnp.int32, (256, 256), 0)
    c = lax.broadcasted_iota(jnp.int32, (256, 256), 1)
    return jnp.where((r < rank) & (c < rank), gram, jnp.where(r == c, 1.0, 0.0))


def row_masked(a, rank):
    return jnp.where(lax.broadcasted_iota(jnp.int32, a.shape, 0) < rank, a, 0.0)


def col_masked(a, rank):
    return jnp.where(lax.broadcasted_iota(jnp.int32, a.shape, 1) < rank, a, 0.0)


def far_first(i):
    return lax.rem(2 + 3 * i + 3 * lax.div(i * (i - 1), 2), 4)


AROUND = ((2, 2), (2, 1), (2, 3), (1, 2), (3, 2), (1, 1), (3, 3), (1, 3), (3, 1), (2, 0), (0, 2), (1, 0), (3, 0), (0, 1), (0, 3))
BY_SOURCE = ((2, 2), (2, 1), (2, 3), (2, 0), (1, 2), (3, 2), (1, 1), (3, 3), (1, 3), (3, 1), (1, 0), (3, 0), (0, 2), (0, 1), (0, 3))


def kernel(ranks, f_hbm, s_hbm, leaf, top, coupling,
           fbuf, sbuf, sh, sl, part, xbuf, outbuf, rbuf, acc, samples, zb, pair, cb, chain, bth, btl, cbuf, hown, hother,
           fsem, ssem, xs_sem, xr_sem, rs_sem, rr_sem, as_sem, ar_sem, ws_sem, wr_sem,
           zs_sem, zr_sem, vs_sem, vr_sem, csem):
    z = lax.axis_index("row")
    me = lax.axis_index("col")
    core = lax.rem(me, 2)
    chip = lax.div(me, 2)
    x = lax.div(chip, 4)
    y = lax.rem(chip, 4)
    sibling = {"row": z, "col": chip * 2 + 1 - core}

    def chip_at(dx, dy):
        return lax.rem(x + dx, 4) * 4 + lax.rem(y + dy, 4)

    def peer(q):
        return {"row": z, "col": q * 2 + core}

    def along_z(step):
        return {"row": z + step * (1 - 2 * lax.rem(lax.div(z, step), 2)), "col": me}

    def chunk_copy(s):
        xs = lax.rem(x + far_first(s), 4)
        return pltpu.make_async_copy(f_hbm.at[pl.ds(pl.multiple_of(xs * 256, 256), 256)], fbuf.at[xs], fsem.at[s])

    def remote(src, dst, send, recv, device):
        return pltpu.make_async_remote_copy(src_ref=src, dst_ref=dst, send_sem=send, recv_sem=recv,
                                            device_id=device, device_id_type=MESH)

    scopy = pltpu.make_async_copy(s_hbm, sbuf, ssem)
    scopy.start()
    for s in range(4):
        chunk_copy(s).start()

    barrier = pltpu.get_barrier_semaphore()
    pl.semaphore_signal(barrier, inc=1, device_id=sibling, device_id_type=MESH)
    for dx, dy in AROUND:
        pl.semaphore_signal(barrier, inc=1, device_id=peer(chip_at(dx, dy)), device_id_type=MESH)
    for step in (1, 2):
        pl.semaphore_signal(barrier, inc=1, device_id=along_z(step), device_id_type=MESH)

    scopy.wait()
    sh[...], sl[...] = split(sbuf[...])
    pl.semaphore_wait(barrier, 18)

    def cores_copy(s):
        return remote(part.at[s, :, 1 - core], xbuf.at[s], xs_sem.at[s], xr_sem.at[s], sibling)

    def shard_copy(s, yy, q):
        return remote(outbuf.at[s, yy], rbuf.at[chip], rs_sem.at[q], rr_sem.at[chip], peer(q))

    @pl.loop(0, 5)
    def _(s):
        @pl.when(s < 4)
        def _():
            chunk_copy(s).wait()
            p = dot3(split(fbuf[lax.rem(x + far_first(s), 4)]), (sh[...], sl[...]))
            part[s] = p.reshape(4, 2, 32, 256)
            cores_copy(s).start()

        @pl.when(s > 0)
        def _():
            t = s - 1
            xt = lax.rem(x + far_first(t), 4)
            cores_copy(t).wait_recv()
            outbuf[t] = part[t, :, core] + xbuf[t]

            @pl.loop(0, 4)
            def _(u):
                yy = lax.rem(y + far_first(u), 4)
                q = xt * 4 + yy

                @pl.when(q != chip)
                def _():
                    shard_copy(t, yy, q).start()

    acc[...] = outbuf[3, y]
    for dx, dy in BY_SOURCE:
        q = chip_at(dx, dy)
        remote(outbuf.at[0, 0], rbuf.at[q], rs_sem.at[q], rr_sem.at[q], peer(q)).wait_recv()
        acc[...] += rbuf[q]

    samples[me] = acc[...]
    chain[...] = acc[...]

    def own_copy(q):
        return remote(samples.at[me], samples.at[me], as_sem.at[q], ar_sem.at[chip], peer(q))

    def relay_copy(q):
        return remote(samples.at[q * 2 + core], samples.at[q * 2 + core], ws_sem.at[q], wr_sem.at[q], sibling)

    for dx, dy in AROUND:
        own_copy(chip_at(dx, dy)).start()
    relay_copy(chip).start()
    for dx, dy in AROUND[::-1]:
        q = chip_at(dx, dy)
        remote(samples.at[me], samples.at[q * 2 + core], as_sem.at[q], ar_sem.at[q], peer(q)).wait_recv()
        relay_copy(q).start()

    @pl.loop(0, 16)
    def _(q):
        remote(samples.at[q * 2 + core], samples.at[q * 2 + 1 - core], ws_sem.at[q], wr_sem.at[q], sibling).wait_recv()

    full = split(samples[...].reshape(1024, 256))
    pair[...] = dot3(full, full, TN)

    def coupling_copy(i):
        cols = pl.ds(pl.multiple_of(i * 256, 256), 256)
        return pltpu.make_async_copy(cbuf.at[:, cols], coupling.at[:, cols], csem.at[i])

    def coupling_tile(i):
        cols = pl.ds(pl.multiple_of(i * 256, 256), 256)
        f = fbuf[:, :, cols].reshape(1024, 256)
        cbuf[:, cols] = dot3((bth[...], btl[...]), split(f))
        coupling_copy(i).start()

    @pl.loop(0, 3)
    def _(level):
        rank = ranks[level, z]
        place(zb, 0, masked(pair[...], rank))
        chol_inverse(zb, 1)
        w = split(taken(zb, 0))
        moved = dot3(split(col_masked(chain[...], rank)), w, NT)
        chain[...] = moved

        @pl.when(level == 0)
        def _():
            leaf[...] = chain[...]

        def z_copy():
            half = pl.ds(pl.multiple_of(core * 192, 64), 192)
            return remote(hown.at[level, half], hother.at[level, half], zs_sem.at[level], zr_sem.at[level],
                          along_z(level + 1))

        def z_relay():
            half = pl.ds(pl.multiple_of(core * 192, 64), 192)
            return remote(hother.at[level, half], hother.at[level, half], vs_sem.at[level], vr_sem.at[level], sibling)

        def z_relay_in():
            half = pl.ds(pl.multiple_of((1 - core) * 192, 64), 192)
            return remote(hother.at[level, half], hother.at[level, half], vs_sem.at[level], vr_sem.at[level], sibling)

        @pl.when(level < 2)
        def _():
            g = pair[...]
            c = split(dot3(w, split(row_masked(g, rank))))
            ct = split(dot3(split(col_masked(g, rank)), w, NT))
            h = dot3(ct, c)
            hown[level, 0:128] = h[:128, :128]
            hown[level, 128:256] = h[128:, :128]
            hown[level, 256:384] = h[128:, 128:]
            z_copy().start()
            pair[...] = h
            cb[0] = c[0]
            cb[1] = c[1]

            @pl.when(level == 0)
            def _():
                bt = dot3(w, split(col_masked(samples[...].reshape(1024, 256), rank)), NT)
                bth[...], btl[...] = split(bt)

            @pl.loop(0, 3)
            def _(i):
                coupling_tile(level * 4 + i)

            z_copy().wait_recv()
            z_relay().start()
            chain[...] = dot3(split(chain[...]), (cb[0], cb[1]))
            coupling_tile(level * 4 + 3)
            z_relay_in().wait_recv()
            o = hother[level]
            across = o[128:256]
            pair[:128, :128] += o[:128]
            pair[128:, :128] += across
            pair[:128, 128:] += across.T
            pair[128:, 128:] += o[256:]
            z_copy().wait_send()
            z_relay().wait_send()

    top[...] = chain[...]

    for s in range(4):
        cores_copy(s).wait_send()
    for dx, dy in AROUND:
        q = chip_at(dx, dy)
        shard_copy(0, 0, q).wait_send()
        own_copy(q).wait_send()

    @pl.loop(0, 16)
    def _(q):
        relay_copy(q).wait_send()

    @pl.loop(0, 8)
    def _(i):
        coupling_copy(i).wait()


def body(frontal, sketch, rank_table):
    vmem = pl.BlockSpec(memory_space=pltpu.VMEM)
    hbm = pl.BlockSpec(memory_space=pltpu.HBM)
    dma = pltpu.SemaphoreType.DMA
    bf16 = jnp.bfloat16
    return pl.pallas_call(
        kernel,
        out_shape=(jax.ShapeDtypeStruct((32, 256), F32), jax.ShapeDtypeStruct((32, 256), F32),
                   jax.ShapeDtypeStruct((256, 2048), F32)),
        in_specs=[pl.BlockSpec(memory_space=pltpu.SMEM), hbm, hbm],
        out_specs=(vmem, vmem, hbm),
        scratch_shapes=[
            pltpu.VMEM((4, 256, 2048), F32),
            pltpu.VMEM((2048, 256), F32),
            pltpu.VMEM((2048, 256), bf16),
            pltpu.VMEM((2048, 256), bf16),
            pltpu.VMEM((4, 4, 2, 32, 256), F32),
            pltpu.VMEM((4, 4, 32, 256), F32),
            pltpu.VMEM((4, 4, 32, 256), F32),
            pltpu.VMEM((16, 32, 256), F32),
            pltpu.VMEM((32, 256), F32),
            pltpu.VMEM((32, 32, 256), F32),
            pltpu.VMEM((1, 256, 256), F32),
            pltpu.VMEM((256, 256), F32),
            pltpu.VMEM((2, 256, 256), bf16),
            pltpu.VMEM((32, 256), F32),
            pltpu.VMEM((256, 1024), bf16),
            pltpu.VMEM((256, 1024), bf16),
            pltpu.VMEM((256, 2048), F32),
            pltpu.VMEM((2, 384, 128), F32),
            pltpu.VMEM((2, 384, 128), F32),
            dma((4,)), dma, dma((4,)), dma((4,)),
            dma((16,)), dma((16,)), dma((16,)), dma((16,)), dma((16,)), dma((16,)),
            dma((2,)), dma((2,)), dma((2,)), dma((2,)), dma((8,)),
        ],
        compiler_params=pltpu.CompilerParams(collective_id=0, has_side_effects=True, vmem_limit_bytes=58 * 2**20),
        cost_estimate=pl.CostEstimate(flops=7 * 2**30, bytes_accessed=12 * 2**20, transcendentals=0),
    )(rank_table, frontal, sketch)


def solution(mesh):
    return jax.shard_map(
        body,
        mesh=mesh,
        in_specs=(P("row", "col"), P("col", None), P()),
        out_specs=(P(("row", "col"), None), P(("row", "col"), None), P("row", "col")),
        check_vma=False,
    )
```

time: 398 us -> 72.8 us (0.18); the launches traced: 393 us -> 72.5 us
  other arithmetic: 172 us -> 0 us
  waiting for transfers between devices: 125 us -> 0 us
  Pallas kernels: 0 us -> 66 us
  matrix products: 46.7 us -> 0 us
  local copies, waits for them, and re-layouts: 26.8 us -> 5.88 us
  between operations: 18.8 us -> 0.64 us
    another operation x28 -> x0, other arithmetic: 165 us -> none  [the longest x20 104 us: factor(): return jnp.linalg.cholesky(masked)]
    psum x1 -> x0, waiting for transfers between devices: 113 us -> none  [body(): samples = lax.psum(product(frontal, sketch), 'col')]
    pallas_call x0 -> x1, Pallas kernels: none -> 66 us  [body(): pl.pallas_call(kernel, out_shape=(jax.ShapeDtypeStruct((32, 256), F32), j...]
    dot_general x8 -> x0, matrix products: 29.1 us -> none  [product(): jnp.dot(left, right, precision=lax.Precision.HIGHEST, preferred_element_t...]
    another operation x36 -> x0, local copies, waits for them, and re-layouts: 20 us -> none  [the longest x13 12 us: right_solve(): lax.linalg.triangular_solve(factor_low, operand, left_side=False, lower=T...]
    another operation x21 -> x0, matrix products: 17.5 us -> none  [the longest x6 6.45 us: factor(): return jnp.linalg.cholesky(masked)]
    ppermute x2 -> x0, waiting for transfers between devices: 11.7 us -> none  [swapped(): return lax.ppermute(block, axis, route)]
  transfers between devices with their start and end apart: 3 -> 0, of which waited for: 2 -> 0; matrix products, arithmetic and copies ran while one was open for 6% -> 0% of each run, Pallas kernels for 0% -> 0%
where the time goes in v2:
time: 72.8 us; the launch traced here: 72.5 us
  Pallas kernels  66 us (91%)
  local copies, waits for them, and re-layouts  5.88 us (8%)
    pallas_call x1, Pallas kernels, body(): pl.pallas_call(kernel, out_shape=(jax.ShapeDtypeStruct((32, 256), F32), j...  66 us
    unnamed x3, local copies, waits for them, and re-layouts  5.88 us

profile of v2, /device:TPU:1, one launch (start us, length us, event | category | flops | bytes accessed | tf_op | source)
XLA Modules:
  0.0 72.5 jit_solution(17014271783389647608)
XLA Ops:
  0.6 66.0 %shard_map.58 = (f32[32,256]{1,0:T(8,128)}, f32[32,256]{1,0:T(8,128)}, f32[256,2048]{1,0:T(8,128)}) custom-call(s32[3,8]{1,0:T(4,128)} %ranks.1, f32[1024,2048]{1,0:T(8,128)} %f_hbm.1, f32[2048,256]{1,0:T(8,128)} %s_hbm.1), custom_call_target="tpu_custom_call" | custom-call | flops 7516192768 | bytes 12582912 | tf_op jit(solution)/shard_map/pallas_call | solution.py:389
  66.7 1.4 %copy.9 = f32[32,256]{1,0:T(8,128)} copy(f32[32,256]{1,0:T(8,128)} %get-tuple-element.6) | data formatting | bytes 65536
  68.0 1.4 %copy.10 = f32[32,256]{1,0:T(8,128)} copy(f32[32,256]{1,0:T(8,128)} %get-tuple-element.7) | data formatting | bytes 65536
  69.4 3.1 %copy.11 = f32[256,2048]{1,0:T(8,128)} copy(f32[256,2048]{1,0:T(8,128)} %get-tuple-element.8) | data formatting | bytes 4194304

commit v3 on v2

--- a/solution.py
+++ b/solution.py
@@ -184,10 +184,10 @@
 BY_SOURCE = ((2, 2), (2, 1), (2, 3), (2, 0), (1, 2), (3, 2), (1, 1), (3, 3), (1, 3), (3, 1), (1, 0), (3, 0), (0, 2), (0, 1), (0, 3))
 
 
-def kernel(ranks, f_hbm, s_hbm, leaf, top, coupling,
-           fbuf, sbuf, sh, sl, part, xbuf, outbuf, rbuf, acc, samples, zb, pair, cb, chain, bth, btl, cbuf, hown, hother,
+def kernel(ranks, f_hbm, s_hbm, leaf, coupling, pair, chain,
+           fbuf, sbuf, sh, sl, part, xbuf, outbuf, rbuf, acc, samples, zb, cb, bth, btl, hown, hother,
            fsem, ssem, xs_sem, xr_sem, rs_sem, rr_sem, as_sem, ar_sem, ws_sem, wr_sem,
-           zs_sem, zr_sem, vs_sem, vr_sem, csem):
+           zs_sem, zr_sem, vs_sem, vr_sem):
     z = lax.axis_index("row")
     me = lax.axis_index("col")
     core = lax.rem(me, 2)
@@ -227,7 +227,6 @@
 
     scopy.wait()
     sh[...], sl[...] = split(sbuf[...])
-    pl.semaphore_wait(barrier, 18)
 
     def cores_copy(s):
         return remote(part.at[s, :, 1 - core], xbuf.at[s], xs_sem.at[s], xr_sem.at[s], sibling)
@@ -242,6 +241,11 @@
             chunk_copy(s).wait()
             p = dot3(split(fbuf[lax.rem(x + far_first(s), 4)]), (sh[...], sl[...]))
             part[s] = p.reshape(4, 2, 32, 256)
+
+            @pl.when(s == 0)
+            def _():
+                pl.semaphore_wait(barrier, 18)
+
             cores_copy(s).start()
 
         @pl.when(s > 0)
@@ -290,17 +294,12 @@
     full = split(samples[...].reshape(1024, 256))
     pair[...] = dot3(full, full, TN)
 
-    def coupling_copy(i):
-        cols = pl.ds(pl.multiple_of(i * 256, 256), 256)
-        return pltpu.make_async_copy(cbuf.at[:, cols], coupling.at[:, cols], csem.at[i])
-
     def coupling_tile(i):
         cols = pl.ds(pl.multiple_of(i * 256, 256), 256)
         f = fbuf[:, :, cols].reshape(1024, 256)
-        cbuf[:, cols] = dot3((bth[...], btl[...]), split(f))
-        coupling_copy(i).start()
-
-    @pl.loop(0, 3)
+        coupling[:, cols] = dot3((bth[...], btl[...]), split(f))
+
+    @pl.loop(0, 2)
     def _(level):
         rank = ranks[level, z]
         place(zb, 0, masked(pair[...], rank))
@@ -326,44 +325,40 @@
             half = pl.ds(pl.multiple_of((1 - core) * 192, 64), 192)
             return remote(hother.at[level, half], hother.at[level, half], vs_sem.at[level], vr_sem.at[level], sibling)
 
-        @pl.when(level < 2)
+        g = pair[...]
+        c = split(dot3(w, split(row_masked(g, rank))))
+        ct = split(dot3(split(col_masked(g, rank)), w, NT))
+        h = dot3(ct, c)
+        hown[level, 0:128] = h[:128, :128]
+        hown[level, 128:256] = h[128:, :128]
+        hown[level, 256:384] = h[128:, 128:]
+        z_copy().start()
+        pair[...] = h
+        cb[0] = c[0]
+        cb[1] = c[1]
+
+        @pl.when(level == 0)
         def _():
-            g = pair[...]
-            c = split(dot3(w, split(row_masked(g, rank))))
-            ct = split(dot3(split(col_masked(g, rank)), w, NT))
-            h = dot3(ct, c)
-            hown[level, 0:128] = h[:128, :128]
-            hown[level, 128:256] = h[128:, :128]
-            hown[level, 256:384] = h[128:, 128:]
-            z_copy().start()
-            pair[...] = h
-            cb[0] = c[0]
-            cb[1] = c[1]
-
-            @pl.when(level == 0)
-            def _():
-                bt = dot3(w, split(col_masked(samples[...].reshape(1024, 256), rank)), NT)
-                bth[...], btl[...] = split(bt)
-
-            @pl.loop(0, 3)
-            def _(i):
-                coupling_tile(level * 4 + i)
-
-            z_copy().wait_recv()
-            z_relay().start()
-            chain[...] = dot3(split(chain[...]), (cb[0], cb[1]))
-            coupling_tile(level * 4 + 3)
-            z_relay_in().wait_recv()
-            o = hother[level]
-            across = o[128:256]
-            pair[:128, :128] += o[:128]
-            pair[128:, :128] += across
-            pair[:128, 128:] += across.T
-            pair[128:, 128:] += o[256:]
-            z_copy().wait_send()
-            z_relay().wait_send()
-
-    top[...] = chain[...]
+            bt = dot3(w, split(col_masked(samples[...].reshape(1024, 256), rank)), NT)
+            bth[...], btl[...] = split(bt)
+
+        @pl.loop(0, 3)
+        def _(i):
+            coupling_tile(level * 4 + i)
+
+        z_copy().wait_recv()
+        z_relay().start()
+        chain[...] = dot3(split(chain[...]), (cb[0], cb[1]))
+        coupling_tile(level * 4 + 3)
+        z_relay_in().wait_recv()
+        o = hother[level]
+        across = o[128:256]
+        pair[:128, :128] += o[:128]
+        pair[128:, :128] += across
+        pair[:128, 128:] += across.T
+        pair[128:, 128:] += o[256:]
+        z_copy().wait_send()
+        z_relay().wait_send()
 
     for s in range(4):
         cores_copy(s).wait_send()
@@ -376,9 +371,17 @@
     def _(q):
         relay_copy(q).wait_send()
 
-    @pl.loop(0, 8)
-    def _(i):
-        coupling_copy(i).wait()
+
+def last_kernel(ranks, leaf_in, coupling_in, pair, chain, leaf, top, coupling, zb, sem):
+    copies = [pltpu.make_async_copy(coupling_in, coupling, sem.at[0]), pltpu.make_async_copy(leaf_in, leaf, sem.at[1])]
+    for copy in copies:
+        copy.start()
+    rank = ranks[2, lax.axis_index("row")]
+    place(zb, 0, masked(pair[...], rank))
+    chol_inverse(zb, 1)
+    top[...] = dot3(split(col_masked(chain[...], rank)), split(taken(zb, 0)), NT)
+    for copy in copies:
+        copy.wait()
 
 
 def body(frontal, sketch, rank_table):
@@ -386,12 +389,14 @@
     hbm = pl.BlockSpec(memory_space=pltpu.HBM)
     dma = pltpu.SemaphoreType.DMA
     bf16 = jnp.bfloat16
-    return pl.pallas_call(
+    smem = pl.BlockSpec(memory_space=pltpu.SMEM)
+    frontal = pltpu.with_memory_space_constraint(frontal, pltpu.HBM)
+    sketch = pltpu.with_memory_space_constraint(sketch, pltpu.HBM)
+    held = pl.pallas_call(
         kernel,
-        out_shape=(jax.ShapeDtypeStruct((32, 256), F32), jax.ShapeDtypeStruct((32, 256), F32),
-                   jax.ShapeDtypeStruct((256, 2048), F32)),
-        in_specs=[pl.BlockSpec(memory_space=pltpu.SMEM), hbm, hbm],
-        out_specs=(vmem, vmem, hbm),
+        out_shape=(pltpu.VMEM((32, 256), F32), pltpu.VMEM((256, 2048), F32), pltpu.VMEM((256, 256), F32), pltpu.VMEM((32, 256), F32)),
+        in_specs=[smem, hbm, hbm],
+        out_specs=(vmem, vmem, vmem, vmem),
         scratch_shapes=[
             pltpu.VMEM((4, 256, 2048), F32),
             pltpu.VMEM((2048, 256), F32),
@@ -404,21 +409,27 @@
             pltpu.VMEM((32, 256), F32),
             pltpu.VMEM((32, 32, 256), F32),
             pltpu.VMEM((1, 256, 256), F32),
-            pltpu.VMEM((256, 256), F32),
             pltpu.VMEM((2, 256, 256), bf16),
-            pltpu.VMEM((32, 256), F32),
             pltpu.VMEM((256, 1024), bf16),
             pltpu.VMEM((256, 1024), bf16),
-            pltpu.VMEM((256, 2048), F32),
             pltpu.VMEM((2, 384, 128), F32),
             pltpu.VMEM((2, 384, 128), F32),
             dma((4,)), dma, dma((4,)), dma((4,)),
             dma((16,)), dma((16,)), dma((16,)), dma((16,)), dma((16,)), dma((16,)),
-            dma((2,)), dma((2,)), dma((2,)), dma((2,)), dma((8,)),
+            dma((2,)), dma((2,)), dma((2,)), dma((2,)),
         ],
-        compiler_params=pltpu.CompilerParams(collective_id=0, has_side_effects=True, vmem_limit_bytes=58 * 2**20),
+        compiler_params=pltpu.CompilerParams(collective_id=0, has_side_effects=True, vmem_limit_bytes=40 * 2**20),
         cost_estimate=pl.CostEstimate(flops=7 * 2**30, bytes_accessed=12 * 2**20, transcendentals=0),
     )(rank_table, frontal, sketch)
+    return pl.pallas_call(
+        last_kernel,
+        out_shape=(jax.ShapeDtypeStruct((32, 256), F32), jax.ShapeDtypeStruct((32, 256), F32),
+                   jax.ShapeDtypeStruct((256, 2048), F32)),
+        in_specs=[smem, vmem, vmem, vmem, vmem],
+        out_specs=(hbm, vmem, hbm),
+        scratch_shapes=[pltpu.VMEM((1, 256, 256), F32), dma((2,))],
+        compiler_params=pltpu.CompilerParams(vmem_limit_bytes=16 * 2**20),
+    )(rank_table, *held)
 
 
 def solution(mesh):

time: 72.8 us -> 67.9 us (0.933)
  local copies, waits for them, and re-layouts: 5.88 us -> 0.67 us
    unnamed x3 -> x2, local copies, waits for them, and re-layouts: 5.88 us -> 0.67 us
    pallas_call x1 -> x2, Pallas kernels: 66 us -> 66.3 us  [the longest x1 59 us: body(): pl.pallas_call(kernel, out_shape=(pltpu.VMEM((32, 256), F32), pltpu.VMEM(...]
where the time goes in v3:
time: 67.9 us; the launch traced here: 67.8 us
  Pallas kernels  66.3 us (98%)
  between operations  0.81 us (1%)
    pallas_call x1, Pallas kernels, body(): pl.pallas_call(kernel, out_shape=(pltpu.VMEM((32, 256), F32), pltpu.VMEM(...  59 us
    pallas_call x1, Pallas kernels, body(): pl.pallas_call(last_kernel, out_shape=(jax.ShapeDtypeStruct((32, 256), F3...  7.33 us

profile of v3, /device:TPU:1, one launch (start us, length us, event | category | flops | bytes accessed | tf_op | source)
XLA Modules:
  0.0 67.8 jit_solution(9042994543238216357)
XLA Ops:
  0.6 0.0 copy-start
  0.6 0.7 copy-done
  1.3 59.0 %shard_map.58 = (f32[32,256]{1,0:T(8,128)S(1)}, f32[256,2048]{1,0:T(8,128)S(1)}, f32[256,256]{1,0:T(8,128)S(1)}, f32[32,256]{1,0:T(8,128)S(1)}) custom-call(s32[3,8]{1,0:T(4,128)S(1)} %copy-done, f32[1024,2048]{1,0:T(8,128)} %f_hbm.1, f32[2048,256]{1,0:T(8,128)} %s_hbm.1), custom_call_target="tpu_custom_call" | custom-call | flops 7516192768 | bytes 12582912 | tf_op jit(solution)/shard_map/pallas_call | solution.py:395
  60.3 7.3 %shard_map.59 = (f32[32,256]{1,0:T(8,128)}, f32[32,256]{1,0:T(8,128)}, f32[256,2048]{1,0:T(8,128)}) custom-call(s32[3,8]{1,0:T(4,128)S(1)} %copy-done, f32[32,256]{1,0:T(8,128)S(1)} %get-tuple-element.7.leaf_in, f32[256,2048]{1,0:T(8,128)S(1)} %get-tuple-element.8.coupling_in, f32[256,256]{1,0:T(8,128)S(1)} %get-tuple-element.9.pair, ...), custom_call_target="tpu_custom_call" | custom-call | tf_op jit(solution)/shard_map/pallas_call | solution.py:424
Async XLA Ops:
  0.6 0.7 %copy-start = (s32[3,8]{1,0:T(4,128)S(1)}, s32[3,8]{1,0:T(4,128)}, u32[]{:S(2)}) copy-start(s32[3,8]{1,0:T(4,128)} %ranks.3) | copy-start | bytes 292

commit v4 on v3

v4 whole, which is shorter than its diff:
```python
import functools

import jax
import jax.numpy as jnp
from jax import lax
from jax.experimental import pallas as pl
from jax.experimental.pallas import tpu as pltpu
from jax.sharding import PartitionSpec as P

MESH = pl.DeviceIdType.MESH
NN = (((1,), (0,)), ((), ()))
NT = (((1,), (1,)), ((), ()))
TN = (((0,), (0,)), ((), ()))
F32 = jnp.float32


def split(x):
    hi = x.astype(jnp.bfloat16)
    return hi, (x - hi.astype(F32)).astype(jnp.bfloat16)


def dot3(a, b, dims=NN):
    ah, al = a if isinstance(a, tuple) else split(a)
    bh, bl = b if isinstance(b, tuple) else split(b)
    d = functools.partial(lax.dot_general, dimension_numbers=dims, preferred_element_type=F32)
    return d(ah, bh) + (d(ah, bl) + d(al, bh))


PB = 32
HALF = 16


def panel_inverse(x, s):
    lane = lax.broadcasted_iota(jnp.int32, (8, 128), 1)
    sub = lax.broadcasted_iota(jnp.int32, (8, 128), 0)
    m = list(x)
    n = [jnp.where(lane == sub + (8 * g + PB * s), 1.0, 0.0).astype(F32) for g in range(4)]
    scale = [jnp.zeros((8, 128), F32) for _ in range(4)]
    coef = [jnp.zeros((8, 128), F32) for _ in range(4)]
    for q in range(2):
        c = {}
        for k in range(HALF):
            for g in range(2 * q, 4):
                at = PB * s + HALF * q + k
                c[k, g] = jnp.take_along_axis(m[g], lane * 0 + at, axis=1)
        for j in range(0, HALF, 2):
            gj = 2 * q + j // 8
            s0 = j % 8

            def row(v, i):
                return jnp.broadcast_to(v[i:i + 1, :], (8, 128))

            a = row(c[j, gj], s0)
            b = row(c[j, gj], s0 + 1)
            d = row(c[j + 1, gj], s0 + 1)
            det = a * d - b * b
            rdet = 1.0 / det
            ra = 1.0 / a
            scale[gj] = jnp.where(sub == s0, lax.rsqrt(a), jnp.where(sub == s0 + 1, lax.rsqrt(det * ra), scale[gj]))
            coef[gj] = jnp.where(sub == s0 + 1, b * ra, coef[gj])
            first = {k: row(c[k, gj], s0) for k in range(j + 2, HALF)}
            second = {k: row(c[k, gj], s0 + 1) for k in range(j + 2, HALF)}
            n0, n1 = row(n[gj], s0), row(n[gj], s0 + 1)
            m0, m1 = row(m[gj], s0), row(m[gj], s0 + 1)
            for g in range(gj, 4):
                if g == gj and s0 == 6:
                    continue
                e = d * c[j, g] - b * c[j + 1, g]
                f = a * c[j + 1, g] - b * c[j, g]
                if g == gj:
                    e = jnp.where(sub > s0 + 1, e, 0.0)
                    f = jnp.where(sub > s0 + 1, f, 0.0)
                e = e * rdet
                f = f * rdet
                for k in range(j + 2, HALF):
                    c[k, g] = c[k, g] - (e * first[k] + f * second[k])
                if q == 0:
                    m[g] = m[g] - (e * m0 + f * m1)
                n[g] = n[g] - (e * n0 + f * n1)
    return [(n[g] - coef[g] * pltpu.roll(n[g], 1, 0)) * scale[g] for g in range(4)]


def chol_inverse(z_ref, between):
    here_lane = lax.broadcasted_iota(jnp.int32, (PB, 128), 1)
    lane96 = lax.broadcasted_iota(jnp.int32, (1, 96), 1)
    zeros = jnp.zeros((PB, 128), jnp.bfloat16)
    d = functools.partial(lax.dot_general, preferred_element_type=F32)
    for s in range(4):
        start = PB * s
        w = jnp.concatenate(panel_inverse([z_ref[start + 8 * g:start + 8 * g + 8, :] for g in range(4)], s), axis=0)
        here = here_lane // PB == s
        wh, wl = split(w)
        rh, rl = split(z_ref[start:start + PB, :])

        def padded(v):
            return jnp.concatenate([zeros] * s + [v] + [zeros] * (3 - s), axis=0)

        u = d(wh, padded(rh), NN) + (d(wl, padded(rh), NN) + d(wh, padded(rl), NN))
        u = jnp.where(here, w, u)
        if s < 3:
            below = slice(start + PB, 128)
            z = z_ref[below, :]
            zh, zl = split(z)
            wh3 = jnp.concatenate([wh] * 3, axis=0)
            wl3 = jnp.concatenate([wl] * 3, axis=0)
            lm = d(jnp.concatenate([zh, zl], axis=1), jnp.concatenate([wh3, wh3], axis=1), NT) + d(zh, wl3, NT)
            lh, ll = split(lm)
            uh, ul = split(u)
            delta = d(jnp.where(lane96 < 64, lh, ll), jnp.concatenate([uh, ul, uh], axis=0), NN)
            z_ref[below, :] = jnp.where(here_lane[:1] // PB == s, 0.0, z) - delta
        z_ref[start:start + PB, :] = u
        between(s)


def lower(a):
    r = lax.broadcasted_iota(jnp.int32, a.shape, 0)
    c = lax.broadcasted_iota(jnp.int32, a.shape, 1)
    return jnp.where(c <= r, a, 0.0)


def nothing(s):
    pass


def schur(z_ref, w11, a21, a22):
    l21 = split(dot3(split(a21), w11, NT))
    z_ref[...] = a22 - dot3(l21, l21, NT)
    return -dot3(l21, w11)


def masked(a, rank, row0, col0):
    r = lax.broadcasted_iota(jnp.int32, a.shape, 0) + row0
    c = lax.broadcasted_iota(jnp.int32, a.shape, 1) + col0
    return jnp.where((r < rank) & (c < rank), a, jnp.where(r == c, 1.0, 0.0))


def row_masked(a, rank):
    return jnp.where(lax.broadcasted_iota(jnp.int32, a.shape, 0) < rank, a, 0.0)


def col_masked(a, rank):
    return jnp.where(lax.broadcasted_iota(jnp.int32, a.shape, 1) < rank, a, 0.0)


def far_first(i):
    return lax.rem(2 + 3 * i + 3 * lax.div(i * (i - 1), 2), 4)


AROUND = ((2, 2), (2, 1), (2, 3), (1, 2), (3, 2), (1, 1), (3, 3), (1, 3), (3, 1), (2, 0), (0, 2), (1, 0), (3, 0), (0, 1), (0, 3))
BY_SOURCE = ((2, 2), (2, 1), (2, 3), (2, 0), (1, 2), (3, 2), (1, 1), (3, 3), (1, 3), (3, 1), (1, 0), (3, 0), (0, 2), (0, 1), (0, 3))


def kernel(ranks, f_hbm, s_hbm, leaf, coupling, w11_out, pair, chain,
           fbuf, sbuf, sh, sl, part, xbuf, outbuf, rbuf, acc, samples, zb, wb, gb, cb, bth, btl, hown, hother,
           fsem, ssem, xs_sem, xr_sem, rs_sem, rr_sem, as_sem, ar_sem, ws_sem, wr_sem,
           zs_sem, zr_sem, vs_sem, vr_sem):
    z = lax.axis_index("row")
    me = lax.axis_index("col")
    core = lax.rem(me, 2)
    chip = lax.div(me, 2)
    x = lax.div(chip, 4)
    y = lax.rem(chip, 4)
    sibling = {"row": z, "col": chip * 2 + 1 - core}

    def chip_at(dx, dy):
        return lax.rem(x + dx, 4) * 4 + lax.rem(y + dy, 4)

    def peer(q):
        return {"row": z, "col": q * 2 + core}

    def along_z(step):
        return {"row": z + step * (1 - 2 * lax.rem(lax.div(z, step), 2)), "col": me}

    def chunk_copy(s):
        xs = lax.rem(x + far_first(s), 4)
        return pltpu.make_async_copy(f_hbm.at[pl.ds(pl.multiple_of(xs * 256, 256), 256)], fbuf.at[xs], fsem.at[s])

    def remote(src, dst, send, recv, device):
        return pltpu.make_async_remote_copy(src_ref=src, dst_ref=dst, send_sem=send, recv_sem=recv,
                                            device_id=device, device_id_type=MESH)

    scopy = pltpu.make_async_copy(s_hbm, sbuf, ssem)
    scopy.start()
    for s in range(4):
        chunk_copy(s).start()

    barrier = pltpu.get_barrier_semaphore()
    pl.semaphore_signal(barrier, inc=1, device_id=sibling, device_id_type=MESH)
    for dx, dy in AROUND:
        pl.semaphore_signal(barrier, inc=1, device_id=peer(chip_at(dx, dy)), device_id_type=MESH)
    for step in (1, 2):
        pl.semaphore_signal(barrier, inc=1, device_id=along_z(step), device_id_type=MESH)

    scopy.wait()
    sh[...], sl[...] = split(sbuf[...])

    def cores_copy(s):
        return remote(part.at[s, :, 1 - core], xbuf.at[s], xs_sem.at[s], xr_sem.at[s], sibling)

    def shard_copy(s, yy, q):
        return remote(outbuf.at[s, yy], rbuf.at[chip], rs_sem.at[q], rr_sem.at[chip], peer(q))

    @pl.loop(0, 5)
    def _(s):
        @pl.when(s < 4)
        def _():
            chunk_copy(s).wait()
            p = dot3(split(fbuf[lax.rem(x + far_first(s), 4)]), (sh[...], sl[...]))
            part[s] = p.reshape(4, 2, 32, 256)

            @pl.when(s == 0)
            def _():
                pl.semaphore_wait(barrier, 18)

            cores_copy(s).start()

        @pl.when(s > 0)
        def _():
            t = s - 1
            xt = lax.rem(x + far_first(t), 4)
            cores_copy(t).wait_recv()
            outbuf[t] = part[t, :, core] + xbuf[t]

            @pl.loop(0, 4)
            def _(u):
                yy = lax.rem(y + far_first(u), 4)
                q = xt * 4 + yy

                @pl.when(q != chip)
                def _():
                    shard_copy(t, yy, q).start()

    acc[...] = outbuf[3, y]
    for dx, dy in BY_SOURCE:
        q = chip_at(dx, dy)
        remote(outbuf.at[0, 0], rbuf.at[q], rs_sem.at[q], rr_sem.at[q], peer(q)).wait_recv()
        acc[...] += rbuf[q]

    chain[...] = acc[...]
    for h in range(2):
        samples[h, me] = acc[:, 128 * h:128 * h + 128]

    def own_copy(h, q):
        return remote(samples.at[h, me], samples.at[h, me], as_sem.at[h, q], ar_sem.at[h, chip], peer(q))

    def relay_copy(h, q):
        return remote(samples.at[h, q * 2 + core], samples.at[h, q * 2 + core], ws_sem.at[h, q], wr_sem.at[h, q], sibling)

    for h in range(2):
        for dx, dy in AROUND:
            own_copy(h, chip_at(dx, dy)).start()
        relay_copy(h, chip).start()

    def relay_half(h):
        for dx, dy in AROUND[::-1]:
            q = chip_at(dx, dy)
            remote(samples.at[h, me], samples.at[h, q * 2 + core], as_sem.at[h, q], ar_sem.at[h, q], peer(q)).wait_recv()
            relay_copy(h, q).start()

    def half_arrived(h):
        @pl.loop(0, 16)
        def _(q):
            remote(samples.at[h, q * 2 + core], samples.at[h, q * 2 + 1 - core], ws_sem.at[h, q], wr_sem.at[h, q],
                   sibling).wait_recv()

    def half_samples(h):
        return split(samples[h].reshape(1024, 128))

    def rows_of(piece, c):
        if piece == 0:
            return pl.ds(pl.multiple_of(c * 64, 64), 64)
        return pl.ds(pl.multiple_of(128 + c * 128, 128), 128)

    def z_copy(level, piece):
        at = rows_of(piece, core)
        i = level * 2 + piece
        return remote(hown.at[level, at], hother.at[level, at], zs_sem.at[i], zr_sem.at[i], along_z(level + 1))

    def z_relay(level, piece, c):
        at = rows_of(piece, c)
        i = level * 2 + piece
        return remote(hother.at[level, at], hother.at[level, at], vs_sem.at[i], vr_sem.at[i], sibling)

    relay_half(0)
    half_arrived(0)
    first = half_samples(0)
    pair[0] = dot3(first, first, TN)

    def coupling_tile(i):
        cols = pl.ds(pl.multiple_of(i * 256, 256), 256)
        f = fbuf[:, :, cols].reshape(1024, 256)
        coupling[:, cols] = dot3((bth[...], btl[...]), split(f))

    @pl.loop(0, 3)
    def _(level):
        rank = ranks[level, z]
        zb[...] = masked(pair[0], rank, 0, 0)

        def between(s):
            if s == 1:
                @pl.when(level == 0)
                def _():
                    relay_half(1)

                @pl.when(level > 0)
                def _():
                    z_copy(level - 1, 1).wait_recv()
                    z_relay(level - 1, 1, core).start()

        chol_inverse(zb, between)
        w11_out[...] = lower(zb[...])

        @pl.when(level == 0)
        def _():
            half_arrived(1)
            left, right = half_samples(0), half_samples(1)
            pair[1] = dot3(right, left, TN)
            pair[2] = dot3(right, right, TN)

        @pl.when(level > 0)
        def _():
            z_relay(level - 1, 1, 1 - core).wait_recv()
            pair[1] += hother[level - 1, 128:256]
            pair[2] += hother[level - 1, 256:384]
            for piece in range(2):
                z_copy(level - 1, piece).wait_send()
                z_relay(level - 1, piece, core).wait_send()

        @pl.when(level < 2)
        def _():
            w11 = w11_out[...]
            m21 = schur(zb, split(w11), masked(pair[1], rank, 128, 0), masked(pair[2], rank, 128, 128))
            gb[:128, :128] = pair[0]
            gb[:128, 128:] = pair[1].T
            gb[128:, :128] = pair[1]
            gb[128:, 128:] = pair[2]
            chol_inverse(zb, nothing)
            w22 = lower(zb[...])
            wb[:128, :128] = w11
            wb[:128, 128:] = jnp.zeros((128, 128), F32)
            wb[128:, :128] = dot3(w22, m21)
            wb[128:, 128:] = w22
            w = split(wb[...])
            g = gb[...]
            c = split(dot3(w, split(row_masked(g, rank))))
            ct = split(dot3(split(col_masked(g, rank)), w, NT))

            def block(i, j):
                a, b = slice(128 * i, 128 * i + 128), slice(128 * j, 128 * j + 128)
                return dot3((ct[0][a], ct[1][a]), (c[0][:, b], c[1][:, b]))

            h11 = block(0, 0)
            hown[level, 0:128] = h11
            z_copy(level, 0).start()
            h21, h22 = block(1, 0), block(1, 1)
            hown[level, 128:256] = h21
            hown[level, 256:384] = h22
            z_copy(level, 1).start()
            pair[0] = h11
            pair[1] = h21
            pair[2] = h22
            cb[0] = c[0]
            cb[1] = c[1]
            moved = dot3(split(col_masked(chain[...], rank)), w, NT)
            chain[...] = moved

            @pl.when(level == 0)
            def _():
                leaf[...] = chain[...]
                w0 = split(wb[...])
                whole = col_masked(jnp.concatenate([samples[0].reshape(1024, 128), samples[1].reshape(1024, 128)], axis=1), rank)
                bth[...], btl[...] = split(dot3(w0, split(whole), NT))

            @pl.loop(0, 3)
            def _(i):
                coupling_tile(level * 4 + i)

            z_copy(level, 0).wait_recv()
            z_relay(level, 0, core).start()
            chain[...] = dot3(split(chain[...]), (cb[0], cb[1]))
            coupling_tile(level * 4 + 3)
            z_relay(level, 0, 1 - core).wait_recv()
            pair[0] += hother[level, 0:128]

    for s in range(4):
        cores_copy(s).wait_send()
    for dx, dy in AROUND:
        q = chip_at(dx, dy)
        shard_copy(0, 0, q).wait_send()
        own_copy(0, q).wait_send()
        own_copy(1, q).wait_send()

    @pl.loop(0, 16)
    def _(q):
        relay_copy(0, q).wait_send()
        relay_copy(1, q).wait_send()


def last_kernel(ranks, leaf_in, coupling_in, w11, pair, chain, leaf, top, coupling, zb, sem):
    copies = [pltpu.make_async_copy(coupling_in, coupling, sem.at[0]), pltpu.make_async_copy(leaf_in, leaf, sem.at[1])]
    for copy in copies:
        copy.start()
    rank = ranks[2, lax.axis_index("row")]
    w = split(w11[...])
    m21 = split(schur(zb, w, masked(pair[1], rank, 128, 0), masked(pair[2], rank, 128, 128)))
    t = col_masked(chain[...], rank)
    left = split(t[:, :128])
    right = t[:, 128:] + dot3(left, m21, NT)
    chol_inverse(zb, nothing)
    top[:, :128] = dot3(left, w, NT)
    top[:, 128:] = dot3(split(right), split(lower(zb[...])), NT)
    for copy in copies:
        copy.wait()


def body(frontal, sketch, rank_table):
    vmem = pl.BlockSpec(memory_space=pltpu.VMEM)
    hbm = pl.BlockSpec(memory_space=pltpu.HBM)
    dma = pltpu.SemaphoreType.DMA
    bf16 = jnp.bfloat16
    smem = pl.BlockSpec(memory_space=pltpu.SMEM)
    frontal = pltpu.with_memory_space_constraint(frontal, pltpu.HBM)
    sketch = pltpu.with_memory_space_constraint(sketch, pltpu.HBM)
    held = pl.pallas_call(
        kernel,
        out_shape=(pltpu.VMEM((32, 256), F32), pltpu.VMEM((256, 2048), F32), pltpu.VMEM((128, 128), F32),
                   pltpu.VMEM((3, 128, 128), F32), pltpu.VMEM((32, 256), F32)),
        in_specs=[smem, hbm, hbm],
        out_specs=(vmem,) * 5,
        scratch_shapes=[
            pltpu.VMEM((4, 256, 2048), F32),
            pltpu.VMEM((2048, 256), F32),
            pltpu.VMEM((2048, 256), bf16),
            pltpu.VMEM((2048, 256), bf16),
            pltpu.VMEM((4, 4, 2, 32, 256), F32),
            pltpu.VMEM((4, 4, 32, 256), F32),
            pltpu.VMEM((4, 4, 32, 256), F32),
            pltpu.VMEM((16, 32, 256), F32),
            pltpu.VMEM((32, 256), F32),
            pltpu.VMEM((2, 32, 32, 128), F32),
            pltpu.VMEM((128, 128), F32),
            pltpu.VMEM((256, 256), F32),
            pltpu.VMEM((256, 256), F32),
            pltpu.VMEM((2, 256, 256), bf16),
            pltpu.VMEM((256, 1024), bf16),
            pltpu.VMEM((256, 1024), bf16),
            pltpu.VMEM((2, 384, 128), F32),
            pltpu.VMEM((2, 384, 128), F32),
            dma((4,)), dma, dma((4,)), dma((4,)),
            dma((16,)), dma((16,)), dma((2, 16)), dma((2, 16)), dma((2, 16)), dma((2, 16)),
            dma((4,)), dma((4,)), dma((4,)), dma((4,)),
        ],
        compiler_params=pltpu.CompilerParams(collective_id=0, has_side_effects=True, vmem_limit_bytes=40 * 2**20),
        cost_estimate=pl.CostEstimate(flops=7 * 2**30, bytes_accessed=12 * 2**20, transcendentals=0),
    )(rank_table, frontal, sketch)
    return pl.pallas_call(
        last_kernel,
        out_shape=(jax.ShapeDtypeStruct((32, 256), F32), jax.ShapeDtypeStruct((32, 256), F32),
                   jax.ShapeDtypeStruct((256, 2048), F32)),
        in_specs=[smem] + [vmem] * 5,
        out_specs=(hbm, vmem, hbm),
        scratch_shapes=[pltpu.VMEM((128, 128), F32), dma((2,))],
        compiler_params=pltpu.CompilerParams(vmem_limit_bytes=16 * 2**20),
    )(rank_table, *held)


def solution(mesh):
    return jax.shard_map(
        body,
        mesh=mesh,
        in_specs=(P("row", "col"), P("col", None), P()),
        out_specs=(P(("row", "col"), None), P(("row", "col"), None), P("row", "col")),
        check_vma=False,
    )
```

time: 67.9 us -> 65.2 us (0.960)
  Pallas kernels: 66.3 us -> 63.7 us
    pallas_call x1, Pallas kernels: 7.33 us -> 4.71 us  [body(): pl.pallas_call(last_kernel, out_shape=(jax.ShapeDtypeStruct((32, 256), F3...]
where the time goes in v4:
time: 65.2 us; the launch traced here: 65.1 us
  Pallas kernels  63.7 us (98%)
  local copies, waits for them, and re-layouts  0.67 us (1%)
    pallas_call x1, Pallas kernels, body(): pl.pallas_call(kernel, out_shape=(pltpu.VMEM((32, 256), F32), pltpu.VMEM(...  59 us
    pallas_call x1, Pallas kernels, body(): pl.pallas_call(last_kernel, out_shape=(jax.ShapeDtypeStruct((32, 256), F3...  4.71 us

profile of v4, /device:TPU:1, one launch (start us, length us, event | category | flops | bytes accessed | tf_op | source)
XLA Modules:
  0.0 65.1 jit_solution(10918909174508387397)
XLA Ops:
  0.6 0.0 copy-start
  0.6 0.7 %copy-done = s32[3,8]{1,0:T(4,128)S(1)} copy-done((s32[3,8]{1,0:T(4,128)S(1)}, s32[3,8]{1,0:T(4,128)}, u32[]{:S(2)}) %copy-start) | copy-done | bytes 120
  1.3 59.0 %shard_map.58 = (f32[32,256]{1,0:T(8,128)S(1)}, f32[256,2048]{1,0:T(8,128)S(1)}, f32[128,128]{1,0:T(8,128)S(1)}, f32[3,128,128]{2,1,0:T(8,128)S(1)}, f32[32,256]{1,0:T(8,128)S(1)}) custom-call(s32[3,8]{1,0:T(4,128)S(1)} %copy-done, f32[1024,2048]{1,0:T(8,128)} %f_hbm.1, f32[2048,256]{1,0:T(8,128)} %s_hbm.1), custom_call_target="tpu_custom_call" | custom-call | flops 7516192768 | bytes 12582912 | tf_op jit(solution)/shard_map/pallas_call | solution.py:424
  60.4 4.7 %shard_map.59 = (f32[32,256]{1,0:T(8,128)}, f32[32,256]{1,0:T(8,128)}, f32[256,2048]{1,0:T(8,128)}) custom-call(s32[3,8]{1,0:T(4,128)S(1)} %copy-done, f32[32,256]{1,0:T(8,128)S(1)} %get-tuple-element.8.leaf_in, f32[256,2048]{1,0:T(8,128)S(1)} %get-tuple-element.9.coupling_in, f32[128,128]{1,0:T(8,128)S(1)} %get-tuple-element.10.w11, ...), custom_call_target="tpu_custom_call" | custom-call | tf_op jit(solution)/shard_map/pallas_call | solution.py:456
Async XLA Ops:
  0.6 0.7 %copy-start = (s32[3,8]{1,0:T(4,128)S(1)}, s32[3,8]{1,0:T(4,128)}, u32[]{:S(2)}) copy-start(s32[3,8]{1,0:T(4,128)} %ranks.3) | copy-start | bytes 292

commit v5 on v4

--- a/solution.py
+++ b/solution.py
@@ -74,40 +74,22 @@
                 f = f * rdet
                 for k in range(j + 2, HALF):
                     c[k, g] = c[k, g] - (e * first[k] + f * second[k])
-                if q == 0:
-                    m[g] = m[g] - (e * m0 + f * m1)
+                m[g] = m[g] - (e * m0 + f * m1)
                 n[g] = n[g] - (e * n0 + f * n1)
-    return [(n[g] - coef[g] * pltpu.roll(n[g], 1, 0)) * scale[g] for g in range(4)]
+    return [[(v[g] - coef[g] * pltpu.roll(v[g], 1, 0)) * scale[g] for g in range(4)] for v in (n, m)]
 
 
 def chol_inverse(z_ref, between):
     here_lane = lax.broadcasted_iota(jnp.int32, (PB, 128), 1)
-    lane96 = lax.broadcasted_iota(jnp.int32, (1, 96), 1)
-    zeros = jnp.zeros((PB, 128), jnp.bfloat16)
-    d = functools.partial(lax.dot_general, preferred_element_type=F32)
     for s in range(4):
         start = PB * s
-        w = jnp.concatenate(panel_inverse([z_ref[start + 8 * g:start + 8 * g + 8, :] for g in range(4)], s), axis=0)
+        w, u = panel_inverse([z_ref[start + 8 * g:start + 8 * g + 8, :] for g in range(4)], s)
         here = here_lane // PB == s
-        wh, wl = split(w)
-        rh, rl = split(z_ref[start:start + PB, :])
-
-        def padded(v):
-            return jnp.concatenate([zeros] * s + [v] + [zeros] * (3 - s), axis=0)
-
-        u = d(wh, padded(rh), NN) + (d(wl, padded(rh), NN) + d(wh, padded(rl), NN))
-        u = jnp.where(here, w, u)
+        u = jnp.where(here, jnp.concatenate(w, axis=0), jnp.concatenate(u, axis=0))
         if s < 3:
             below = slice(start + PB, 128)
-            z = z_ref[below, :]
-            zh, zl = split(z)
-            wh3 = jnp.concatenate([wh] * 3, axis=0)
-            wl3 = jnp.concatenate([wl] * 3, axis=0)
-            lm = d(jnp.concatenate([zh, zl], axis=1), jnp.concatenate([wh3, wh3], axis=1), NT) + d(zh, wl3, NT)
-            lh, ll = split(lm)
-            uh, ul = split(u)
-            delta = d(jnp.where(lane96 < 64, lh, ll), jnp.concatenate([uh, ul, uh], axis=0), NN)
-            z_ref[below, :] = jnp.where(here_lane[:1] // PB == s, 0.0, z) - delta
+            lm = split(u.T[below])
+            z_ref[below, :] = jnp.where(here_lane[:1] // PB == s, 0.0, z_ref[below, :]) - dot3(lm, split(u))
         z_ref[start:start + PB, :] = u
         between(s)
 
@@ -276,6 +258,10 @@
         i = level * 2 + piece
         return remote(hown.at[level, at], hother.at[level, at], zs_sem.at[i], zr_sem.at[i], along_z(level + 1))
 
+    def z_direct():
+        at = pl.ds(0, 128)
+        return remote(hown.at[0, at], hother.at[0, at], zs_sem.at[0], zr_sem.at[0], along_z(1))
+
     def z_relay(level, piece, c):
         at = rows_of(piece, c)
         i = level * 2 + piece
@@ -322,9 +308,8 @@
             z_relay(level - 1, 1, 1 - core).wait_recv()
             pair[1] += hother[level - 1, 128:256]
             pair[2] += hother[level - 1, 256:384]
-            for piece in range(2):
-                z_copy(level - 1, piece).wait_send()
-                z_relay(level - 1, piece, core).wait_send()
+            z_copy(level - 1, 1).wait_send()
+            z_relay(level - 1, 1, core).wait_send()
 
         @pl.when(level < 2)
         def _():
@@ -351,7 +336,15 @@
 
             h11 = block(0, 0)
             hown[level, 0:128] = h11
-            z_copy(level, 0).start()
+
+            @pl.when(level == 0)
+            def _():
+                z_direct().start()
+
+            @pl.when(level == 1)
+            def _():
+                z_copy(1, 0).start()
+
             h21, h22 = block(1, 0), block(1, 1)
             hown[level, 128:256] = h21
             hown[level, 256:384] = h22
@@ -371,15 +364,24 @@
                 whole = col_masked(jnp.concatenate([samples[0].reshape(1024, 128), samples[1].reshape(1024, 128)], axis=1), rank)
                 bth[...], btl[...] = split(dot3(w0, split(whole), NT))
 
-            @pl.loop(0, 3)
+            @pl.loop(0, 4)
             def _(i):
                 coupling_tile(level * 4 + i)
 
-            z_copy(level, 0).wait_recv()
-            z_relay(level, 0, core).start()
             chain[...] = dot3(split(chain[...]), (cb[0], cb[1]))
-            coupling_tile(level * 4 + 3)
-            z_relay(level, 0, 1 - core).wait_recv()
+
+            @pl.when(level == 0)
+            def _():
+                z_direct().wait()
+
+            @pl.when(level == 1)
+            def _():
+                z_copy(1, 0).wait()
+                relay = z_relay(1, 0, core)
+                relay.start()
+                z_relay(1, 0, 1 - core).wait_recv()
+                relay.wait_send()
+
             pair[0] += hother[level, 0:128]
 
     for s in range(4):
@@ -421,6 +423,7 @@
     smem = pl.BlockSpec(memory_space=pltpu.SMEM)
     frontal = pltpu.with_memory_space_constraint(frontal, pltpu.HBM)
     sketch = pltpu.with_memory_space_constraint(sketch, pltpu.HBM)
+    rank_table = pltpu.with_memory_space_constraint(rank_table, pltpu.HBM)
     held = pl.pallas_call(
         kernel,
         out_shape=(pltpu.VMEM((32, 256), F32), pltpu.VMEM((256, 2048), F32), pltpu.VMEM((128, 128), F32),

time: 65.2 us -> 63.6 us (0.975)
  Pallas kernels: 63.7 us -> 62.8 us
  local copies, waits for them, and re-layouts: 0.67 us -> 0 us
    pallas_call x1, Pallas kernels: 59 us -> 58.3 us  [body(): pl.pallas_call(kernel, out_shape=(pltpu.VMEM((32, 256), F32), pltpu.VMEM(...]
    unnamed x2 -> x0, local copies, waits for them, and re-layouts: 0.67 us -> none
where the time goes in v5:
time: 63.6 us; the launch traced here: 63.5 us
  Pallas kernels  62.8 us (99%)
  between operations  0.64 us (1%)
    pallas_call x1, Pallas kernels, body(): pl.pallas_call(kernel, out_shape=(pltpu.VMEM((32, 256), F32), pltpu.VMEM(...  58.3 us
    pallas_call x1, Pallas kernels, body(): pl.pallas_call(last_kernel, out_shape=(jax.ShapeDtypeStruct((32, 256), F3...  4.56 us

profile of v5, /device:TPU:1, one launch (start us, length us, event | category | flops | bytes accessed | tf_op | source)
XLA Modules:
  0.0 63.5 jit_solution(570527723746841675)
XLA Ops:
  0.6 58.3 %shard_map.58 = (f32[32,256]{1,0:T(8,128)S(1)}, f32[256,2048]{1,0:T(8,128)S(1)}, f32[128,128]{1,0:T(8,128)S(1)}, f32[3,128,128]{2,1,0:T(8,128)S(1)}, f32[32,256]{1,0:T(8,128)S(1)}) custom-call(s32[3,8]{1,0:T(4,128)} %ranks.3, f32[1024,2048]{1,0:T(8,128)} %f_hbm.1, f32[2048,256]{1,0:T(8,128)} %s_hbm.1), custom_call_target="tpu_custom_call" | custom-call | flops 7516192768 | bytes 12582912 | tf_op jit(solution)/shard_map/pallas_call | solution.py:427
  58.9 4.6 %shard_map.59 = (f32[32,256]{1,0:T(8,128)}, f32[32,256]{1,0:T(8,128)}, f32[256,2048]{1,0:T(8,128)}) custom-call(s32[3,8]{1,0:T(4,128)} %ranks.3, f32[32,256]{1,0:T(8,128)S(1)} %get-tuple-element.8.leaf_in, f32[256,2048]{1,0:T(8,128)S(1)} %get-tuple-element.9.coupling_in, f32[128,128]{1,0:T(8,128)S(1)} %get-tuple-element.10.w11, ...), custom_call_target="tpu_custom_call" | custom-call | tf_op jit(solution)/shard_map/pallas_call | solution.py:459

commit v6 on v5

--- a/solution.py
+++ b/solution.py
@@ -133,7 +133,7 @@
 
 
 def kernel(ranks, f_hbm, s_hbm, leaf, coupling, w11_out, pair, chain,
-           fbuf, sbuf, sh, sl, part, xbuf, outbuf, rbuf, acc, samples, zb, wb, gb, cb, bth, btl, hown, hother,
+           fbuf, sbuf, sh, sl, part, xbuf, outbuf, rbuf, acc, samples, zb, wb, gb, hb, cb, bth, btl, hown, hother,
            fsem, ssem, xs_sem, xr_sem, rs_sem, rr_sem, as_sem, ar_sem, ws_sem, wr_sem,
            zs_sem, zr_sem, vs_sem, vr_sem):
     z = lax.axis_index("row")
@@ -319,20 +319,25 @@
             gb[:128, 128:] = pair[1].T
             gb[128:, :128] = pair[1]
             gb[128:, 128:] = pair[2]
+            g = gb[...]
+            gr = row_masked(g, rank)
+            gc = col_masked(g, rank)
+            w1, m2 = split(w11), split(m21)
+            gr1, gc1 = split(gr[:128]), split(gc[:, :128])
+            c1 = split(dot3(w1, gr1))
+            ct1 = split(dot3(gc1, w1, NT))
+            r2 = split(gr[128:] + dot3(m2, gr1))
+            rt2 = split(gc[:, 128:] + dot3(gc1, m2, NT))
+            hb[...] = dot3(ct1, c1)
             chol_inverse(zb, nothing)
             w22 = lower(zb[...])
-            wb[:128, :128] = w11
-            wb[:128, 128:] = jnp.zeros((128, 128), F32)
-            wb[128:, :128] = dot3(w22, m21)
-            wb[128:, 128:] = w22
-            w = split(wb[...])
-            g = gb[...]
-            c = split(dot3(w, split(row_masked(g, rank))))
-            ct = split(dot3(split(col_masked(g, rank)), w, NT))
+            w2 = split(w22)
+            c2 = split(dot3(w2, r2))
+            ct2 = split(dot3(rt2, w2, NT))
 
             def block(i, j):
                 a, b = slice(128 * i, 128 * i + 128), slice(128 * j, 128 * j + 128)
-                return dot3((ct[0][a], ct[1][a]), (c[0][:, b], c[1][:, b]))
+                return hb[a, b] + dot3((ct2[0][a], ct2[1][a]), (c2[0][:, b], c2[1][:, b]))
 
             h11 = block(0, 0)
             hown[level, 0:128] = h11
@@ -352,10 +357,14 @@
             pair[0] = h11
             pair[1] = h21
             pair[2] = h22
-            cb[0] = c[0]
-            cb[1] = c[1]
-            moved = dot3(split(col_masked(chain[...], rank)), w, NT)
-            chain[...] = moved
+            for i in range(2):
+                cb[i, :128] = c1[i]
+                cb[i, 128:] = c2[i]
+            wb[:128, :128] = w11
+            wb[:128, 128:] = jnp.zeros((128, 128), F32)
+            wb[128:, :128] = dot3(w2, m2)
+            wb[128:, 128:] = w22
+            chain[...] = dot3(split(col_masked(chain[...], rank)), split(wb[...]), NT)
 
             @pl.when(level == 0)
             def _():
@@ -364,9 +373,15 @@
                 whole = col_masked(jnp.concatenate([samples[0].reshape(1024, 128), samples[1].reshape(1024, 128)], axis=1), rank)
                 bth[...], btl[...] = split(dot3(w0, split(whole), NT))
 
-            @pl.loop(0, 4)
+            @pl.loop(0, 3)
             def _(i):
-                coupling_tile(level * 4 + i)
+                coupling_tile(level * 3 + i)
+
+            @pl.when(level == 1)
+            def _():
+                @pl.loop(6, 8)
+                def _(i):
+                    coupling_tile(i)
 
             chain[...] = dot3(split(chain[...]), (cb[0], cb[1]))
 
@@ -444,6 +459,7 @@
             pltpu.VMEM((128, 128), F32),
             pltpu.VMEM((256, 256), F32),
             pltpu.VMEM((256, 256), F32),
+            pltpu.VMEM((256, 256), F32),
             pltpu.VMEM((2, 256, 256), bf16),
             pltpu.VMEM((256, 1024), bf16),
             pltpu.VMEM((256, 1024), bf16),

time: 63.6 us -> 62.3 us (0.980)
  Pallas kernels: 62.8 us -> 61.6 us
    pallas_call x1, Pallas kernels: 58.3 us -> 57 us  [body(): pl.pallas_call(kernel, out_shape=(pltpu.VMEM((32, 256), F32), pltpu.VMEM(...]
where the time goes in v6:
time: 62.3 us; the launch traced here: 62.2 us
  Pallas kernels  61.6 us (99%)
  between operations  0.64 us (1%)
    pallas_call x1, Pallas kernels, body(): pl.pallas_call(kernel, out_shape=(pltpu.VMEM((32, 256), F32), pltpu.VMEM(...  57 us
    pallas_call x1, Pallas kernels, body(): pl.pallas_call(last_kernel, out_shape=(jax.ShapeDtypeStruct((32, 256), F3...  4.57 us

profile of v6, /device:TPU:1, one launch (start us, length us, event | category | flops | bytes accessed | tf_op | source)
XLA Modules:
  0.0 62.2 jit_solution(17318442981427653221)
XLA Ops:
  0.6 57.0 %shard_map.58 = (f32[32,256]{1,0:T(8,128)S(1)}, f32[256,2048]{1,0:T(8,128)S(1)}, f32[128,128]{1,0:T(8,128)S(1)}, f32[3,128,128]{2,1,0:T(8,128)S(1)}, f32[32,256]{1,0:T(8,128)S(1)}) custom-call(s32[3,8]{1,0:T(4,128)} %ranks.3, f32[1024,2048]{1,0:T(8,128)} %f_hbm.1, f32[2048,256]{1,0:T(8,128)} %s_hbm.1), custom_call_target="tpu_custom_call" | custom-call | flops 7516192768 | bytes 12582912 | tf_op jit(solution)/shard_map/pallas_call | solution.py:442
  57.7 4.6 %shard_map.59 = (f32[32,256]{1,0:T(8,128)}, f32[32,256]{1,0:T(8,128)}, f32[256,2048]{1,0:T(8,128)}) custom-call(s32[3,8]{1,0:T(4,128)} %ranks.3, f32[32,256]{1,0:T(8,128)S(1)} %get-tuple-element.8.leaf_in, f32[256,2048]{1,0:T(8,128)S(1)} %get-tuple-element.9.coupling_in, f32[128,128]{1,0:T(8,128)S(1)} %get-tuple-element.10.w11, ...), custom_call_target="tpu_custom_call" | custom-call | tf_op jit(solution)/shard_map/pallas_call | solution.py:475

commit v7 on v6

--- a/solution.py
+++ b/solution.py
@@ -373,27 +373,32 @@
                 whole = col_masked(jnp.concatenate([samples[0].reshape(1024, 128), samples[1].reshape(1024, 128)], axis=1), rank)
                 bth[...], btl[...] = split(dot3(w0, split(whole), NT))
 
-            @pl.loop(0, 3)
+            @pl.loop(0, 2)
             def _(i):
-                coupling_tile(level * 3 + i)
+                coupling_tile(level * 2 + i)
 
             @pl.when(level == 1)
             def _():
+                @pl.loop(4, 6)
+                def _(i):
+                    coupling_tile(i)
+
+            chain[...] = dot3(split(chain[...]), (cb[0], cb[1]))
+
+            @pl.when(level == 0)
+            def _():
+                z_direct().wait()
+
+            @pl.when(level == 1)
+            def _():
+                z_copy(1, 0).wait()
+                relay = z_relay(1, 0, core)
+                relay.start()
+
                 @pl.loop(6, 8)
                 def _(i):
                     coupling_tile(i)
 
-            chain[...] = dot3(split(chain[...]), (cb[0], cb[1]))
-
-            @pl.when(level == 0)
-            def _():
-                z_direct().wait()
-
-            @pl.when(level == 1)
-            def _():
-                z_copy(1, 0).wait()
-                relay = z_relay(1, 0, core)
-                relay.start()
                 z_relay(1, 0, 1 - core).wait_recv()
                 relay.wait_send()
 

time: 62.3 us -> 62.1 us (level)
  no operation moved by 1% of the time
where the time goes in v7:
time: 62.1 us; the launch traced here: 61.9 us
  Pallas kernels  61.3 us (99%)
  between operations  0.64 us (1%)
    pallas_call x1, Pallas kernels, body(): pl.pallas_call(kernel, out_shape=(pltpu.VMEM((32, 256), F32), pltpu.VMEM(...  56.7 us
    pallas_call x1, Pallas kernels, body(): pl.pallas_call(last_kernel, out_shape=(jax.ShapeDtypeStruct((32, 256), F3...  4.57 us

profile of v7, /device:TPU:1, one launch (start us, length us, event | category | flops | bytes accessed | tf_op | source)
XLA Modules:
  0.0 61.9 jit_solution(16763780652318547489)
XLA Ops:
  0.6 56.7 %shard_map.58 = (f32[32,256]{1,0:T(8,128)S(1)}, f32[256,2048]{1,0:T(8,128)S(1)}, f32[128,128]{1,0:T(8,128)S(1)}, f32[3,128,128]{2,1,0:T(8,128)S(1)}, f32[32,256]{1,0:T(8,128)S(1)}) custom-call(s32[3,8]{1,0:T(4,128)} %ranks.3, f32[1024,2048]{1,0:T(8,128)} %f_hbm.1, f32[2048,256]{1,0:T(8,128)} %s_hbm.1), custom_call_target="tpu_custom_call" | custom-call | flops 7516192768 | bytes 12582912 | tf_op jit(solution)/shard_map/pallas_call | solution.py:447
  57.4 4.6 %shard_map.59 = (f32[32,256]{1,0:T(8,128)}, f32[32,256]{1,0:T(8,128)}, f32[256,2048]{1,0:T(8,128)}) custom-call(s32[3,8]{1,0:T(4,128)} %ranks.3, f32[32,256]{1,0:T(8,128)S(1)} %get-tuple-element.8.leaf_in, f32[256,2048]{1,0:T(8,128)S(1)} %get-tuple-element.9.coupling_in, f32[128,128]{1,0:T(8,128)S(1)} %get-tuple-element.10.w11, ...), custom_call_target="tpu_custom_call" | custom-call | tf_op jit(solution)/shard_map/pallas_call | solution.py:480
